TPU v7x, 256 devices: a whole 4x4x8 slice. The times are simulated.
256 devices in a mesh: seq: 32 (over z_lo, y, x), ch: 8 (over z_hi, core).
Axes of the slice: x: 4, y: 4, z: 8 (z_hi: 4, z_lo: 2; z = z_hi * 2 + z_lo), core: 2. Of those that a mesh axis runs over, the one named last changes fastest.
Arguments:
- q_proj: bfloat16 [32768, 4096], P(('seq', 'ch')), may hold values from -6 to 6
- k_proj: bfloat16 [32768, 4096], P(('seq', 'ch')), may hold values from -6 to 6
- v_proj: bfloat16 [32768, 4096], P(('seq', 'ch')), may hold values from -6 to 6
- short_filter: float32 [3, 3, 4096], replicated, may hold values from -3 to 3
- rates: float32 [4096, 16], P('ch'), may hold values from 3.0517578e-05 to 0.03
- residues: float32 [4096, 16], P('ch'), may hold values from -1.5 to 1.5
- skip: float32 [4096], replicated, may hold values from -4 to 4
Outputs:
- mixed: bfloat16 [32768, 4096], P(('seq', 'ch'))
All inputs are finite; a program needn't handle non-finite values.
Results may differ from a plain program's by a relative error of at most 0.008.
Values may be sent and summed in bfloat16 or wider, within the bound.
No kernel may reach another device: no remote copies, remote signals or barrier semaphores. Data moves between devices by JAX's collectives and lax.ppermute only.
A program may use at most 192 MiB of HBM per device.

v0:
```python
import math

import jax
import jax.numpy as jnp
from jax import lax
from jax.sharding import PartitionSpec as P

HIGHEST = lax.Precision.HIGHEST
TWO_PI = 2.0 * math.pi


def shifted(value, axis, steps):
    count = lax.axis_size(axis)
    leading, last = (max(0, -steps), min(count, count - steps))
    return lax.ppermute(value, axis, [(source, source + steps) for source in range(leading, last)])


def widen(value):
    return lax.optimization_barrier(value).astype(jnp.float32)


def short_mix(extended, taps):
    return taps[0] * extended[2:] + taps[1] * extended[1:-1] + taps[2] * extended[:-2]


def filter_values(times, rates, residues):
    weight = residues * jnp.sqrt(-jnp.expm1(-2.0 * rates))

    def add_mode(index, total):
        rate = lax.dynamic_index_in_dim(rates, index, 1, keepdims=False)
        scale = lax.dynamic_index_in_dim(weight, index, 1, keepdims=False)
        return total + scale[None, :] * jnp.exp(-rate[None, :] * times[:, None])

    start = jnp.zeros((times.shape[0], rates.shape[0]), jnp.float32)
    return lax.fori_loop(0, rates.shape[1], add_mode, start)


def phase_table(first, second, period):
    angle = (first[:, None] * second[None, :] % period).astype(jnp.float32) * (TWO_PI / period)
    return (jnp.cos(angle), jnp.sin(angle))


def rows_forward(values, col_start, period):
    row_half, cols, _ = values.shape
    freqs = jnp.arange(2 * row_half, dtype=jnp.int32)
    cos_rows, sin_rows = phase_table(freqs, jnp.arange(row_half, dtype=jnp.int32), 2 * row_half)
    real = jnp.einsum("ka,abc->kbc", cos_rows, values, precision=HIGHEST)
    imag = -jnp.einsum("ka,abc->kbc", sin_rows, values, precision=HIGHEST)
    places = col_start + jnp.arange(cols, dtype=jnp.int32)
    cos_turn, sin_turn = phase_table(freqs, places, period)
    cos_turn = cos_turn[:, :, None]
    sin_turn = sin_turn[:, :, None]
    return (real * cos_turn + imag * sin_turn, imag * cos_turn - real * sin_turn)


def columns_forward(real, imag, span_q):
    count, block, width = real.shape
    span_p = block // span_q
    real = real.reshape(count, span_p, span_q, width)
    imag = imag.reshape(count, span_p, span_q, width)
    cos_p, sin_p = phase_table(
        jnp.arange(span_p, dtype=jnp.int32), jnp.arange(span_p, dtype=jnp.int32), span_p
    )
    first_re = jnp.einsum("jp,kpqc->kjqc", cos_p, real, precision=HIGHEST) + jnp.einsum(
        "jp,kpqc->kjqc", sin_p, imag, precision=HIGHEST
    )
    first_im = jnp.einsum("jp,kpqc->kjqc", cos_p, imag, precision=HIGHEST) - jnp.einsum(
        "jp,kpqc->kjqc", sin_p, real, precision=HIGHEST
    )
    cos_turn, sin_turn = phase_table(
        jnp.arange(span_p, dtype=jnp.int32), jnp.arange(span_q, dtype=jnp.int32), block
    )
    cos_turn = cos_turn[None, :, :, None]
    sin_turn = sin_turn[None, :, :, None]
    turned_re = first_re * cos_turn + first_im * sin_turn
    turned_im = first_im * cos_turn - first_re * sin_turn
    cos_q, sin_q = phase_table(
        jnp.arange(span_q, dtype=jnp.int32), jnp.arange(span_q, dtype=jnp.int32), span_q
    )
    out_re = jnp.einsum("mq,kjqc->kmjc", cos_q, turned_re, precision=HIGHEST) + jnp.einsum(
        "mq,kjqc->kmjc", sin_q, turned_im, precision=HIGHEST
    )
    out_im = jnp.einsum("mq,kjqc->kmjc", cos_q, turned_im, precision=HIGHEST) - jnp.einsum(
        "mq,kjqc->kmjc", sin_q, turned_re, precision=HIGHEST
    )
    return (out_re, out_im)


def columns_inverse(real, imag):
    count, span_q, span_p, width = real.shape
    block = span_p * span_q
    cos_q, sin_q = phase_table(
        jnp.arange(span_q, dtype=jnp.int32), jnp.arange(span_q, dtype=jnp.int32), span_q
    )
    first_re = jnp.einsum("qm,kmjc->kjqc", cos_q, real, precision=HIGHEST) - jnp.einsum(
        "qm,kmjc->kjqc", sin_q, imag, precision=HIGHEST
    )
    first_im = jnp.einsum("qm,kmjc->kjqc", cos_q, imag, precision=HIGHEST) + jnp.einsum(
        "qm,kmjc->kjqc", sin_q, real, precision=HIGHEST
    )
    cos_turn, sin_turn = phase_table(
        jnp.arange(span_p, dtype=jnp.int32), jnp.arange(span_q, dtype=jnp.int32), block
    )
    cos_turn = cos_turn[None, :, :, None]
    sin_turn = sin_turn[None, :, :, None]
    turned_re = first_re * cos_turn - first_im * sin_turn
    turned_im = first_im * cos_turn + first_re * sin_turn
    cos_p, sin_p = phase_table(
        jnp.arange(span_p, dtype=jnp.int32), jnp.arange(span_p, dtype=jnp.int32), span_p
    )
    out_re = jnp.einsum("pj,kjqc->kpqc", cos_p, turned_re, precision=HIGHEST) - jnp.einsum(
        "pj,kjqc->kpqc", sin_p, turned_im, precision=HIGHEST
    )
    out_im = jnp.einsum("pj,kjqc->kpqc", cos_p, turned_im, precision=HIGHEST) + jnp.einsum(
        "pj,kjqc->kpqc", sin_p, turned_re, precision=HIGHEST
    )
    return (out_re.reshape(count, block, width), out_im.reshape(count, block, width))


def twiddle_back(real, imag, row_start, period):
    count, block, _ = real.shape
    freqs = row_start + jnp.arange(count, dtype=jnp.int32)
    cos_turn, sin_turn = phase_table(freqs, jnp.arange(block, dtype=jnp.int32), period)
    cos_turn = cos_turn[:, :, None]
    sin_turn = sin_turn[:, :, None]
    return (real * cos_turn - imag * sin_turn, imag * cos_turn + real * sin_turn)


def rows_inverse(real, imag, row_half):
    freqs = jnp.arange(real.shape[0], dtype=jnp.int32)
    cos_rows, sin_rows = phase_table(jnp.arange(row_half, dtype=jnp.int32), freqs, real.shape[0])
    return jnp.einsum("ak,kbc->abc", cos_rows, real, precision=HIGHEST) - jnp.einsum(
        "ak,kbc->abc", sin_rows, imag, precision=HIGHEST
    )


def convolve_spectra(sig_re, sig_im, fil_re, fil_im):
    return (sig_re * fil_re - sig_im * fil_im, sig_re * fil_im + sig_im * fil_re)


def on_device(q_proj, k_proj, v_proj, short_filter, rates, residues, skip):
    seq_count = lax.axis_size("seq")
    seq_place = lax.axis_index("seq")
    edges = jnp.stack([q_proj[-2:], k_proj[-2:], v_proj[-2:]])
    earlier = shifted(edges, ("seq", "ch"), 1)
    query = short_mix(
        jnp.concatenate([earlier[0], q_proj], axis=0).astype(jnp.float32), short_filter[0]
    ).astype(jnp.bfloat16)
    keyed = short_mix(
        jnp.concatenate([earlier[1], k_proj], axis=0).astype(jnp.float32), short_filter[1]
    )
    valued = short_mix(
        jnp.concatenate([earlier[2], v_proj], axis=0).astype(jnp.float32), short_filter[2]
    )
    signal = (keyed * valued).astype(jnp.bfloat16)
    grouped = lax.all_to_all(signal, "ch", split_axis=1, concat_axis=0, tiled=True)
    block, group_width = grouped.shape
    total_len = block * seq_count
    period = 2 * total_len
    span_q = math.gcd(block, 32)
    col_width = block // seq_count
    col_start = seq_place * col_width
    spread_cols = lax.all_to_all(grouped[None], "seq", split_axis=1, concat_axis=0, tiled=True)
    sig_re, sig_im = rows_forward(spread_cols.astype(jnp.float32), col_start, period)
    sig_re, sig_im = (
        lax.all_to_all(
            sig_re.astype(jnp.bfloat16), "seq", split_axis=0, concat_axis=1, tiled=True
        ).astype(sig_re.dtype),
        lax.all_to_all(
            sig_im.astype(jnp.bfloat16), "seq", split_axis=0, concat_axis=1, tiled=True
        ).astype(sig_im.dtype),
    )
    own_rows = sig_re.shape[0]
    row_start = seq_place * own_rows
    sig_re, sig_im = columns_forward(sig_re, sig_im, span_q)
    times = (seq_place * block + jnp.arange(block, dtype=jnp.int32)).astype(jnp.float32)
    taps = filter_values(times, rates, residues)
    tap_cols = lax.all_to_all(taps[None], "seq", split_axis=1, concat_axis=0, tiled=True)
    fil_re, fil_im = rows_forward(tap_cols, col_start, period)
    fil_re, fil_im = (
        lax.all_to_all(
            fil_re.astype(jnp.bfloat16), "seq", split_axis=0, concat_axis=1, tiled=True
        ).astype(fil_re.dtype),
        lax.all_to_all(
            fil_im.astype(jnp.bfloat16), "seq", split_axis=0, concat_axis=1, tiled=True
        ).astype(fil_im.dtype),
    )
    fil_re, fil_im = columns_forward(fil_re, fil_im, span_q)
    prod_re, prod_im = convolve_spectra(sig_re, sig_im, fil_re, fil_im)
    back_re, back_im = columns_inverse(prod_re, prod_im)
    back_re, back_im = twiddle_back(back_re, back_im, row_start, period)
    back_re, back_im = (
        lax.all_to_all(back_re, "seq", split_axis=1, concat_axis=0, tiled=True),
        lax.all_to_all(back_im, "seq", split_axis=1, concat_axis=0, tiled=True),
    )
    conv_rows = (rows_inverse(back_re, back_im, seq_count) * (1.0 / period)).astype(jnp.bfloat16)
    conv_block = lax.all_to_all(conv_rows, "seq", split_axis=0, concat_axis=1, tiled=True)[0]
    back = lax.all_to_all(conv_block, "ch", split_axis=0, concat_axis=1, tiled=True)
    mixed = widen(query) * (widen(back) + skip[None, :] * widen(signal))
    return mixed.astype(jnp.bfloat16)


def solution(mesh):
    placed = (
        P(("seq", "ch"), None),
        P(("seq", "ch"), None),
        P(("seq", "ch"), None),
        P(),
        P("ch", None),
        P("ch", None),
        P(),
    )
    return jax.shard_map(
        on_device, mesh=mesh, in_specs=placed, out_specs=P(("seq", "ch"), None), check_vma=False
    )
```

profile of v0, /device:TPU:1, one launch (start us, length us, event | category | flops | bytes accessed | tf_op | source)
XLA Modules:
  0.0 639.5 jit_solution(12369880920685844552)
XLA Ops:
  25.7 7.3 %all-to-all-start = ((bf16[128,8,512]{0,2,1:T(8,128)(2,1)}), bf16[128,8,512]{0,2,1:T(8,128)(2,1)S(1)}, u32[]{:S(2)}, u32[]{:S(2)}) async-start(bf16[128,8,512]{0,2,1:T(8,128)(2,1)} %bitcast.17), calls=%async_computation | async-start | bytes 2097152 | tf_op jit(solution)/shard_map/all_to_all | solution.py:156
  33.1 21.4 %all-to-all-done = bf16[128,8,512]{0,2,1:T(8,128)(2,1)S(1)} async-done(((bf16[128,8,512]{0,2,1:T(8,128)(2,1)}), bf16[128,8,512]{0,2,1:T(8,128)(2,1)S(1)}, u32[]{:S(2)}, u32[]{:S(2)}) %all-to-all-start) | async-done | bytes 1048608 | tf_op jit(solution)/shard_map/all_to_all | solution.py:156
  60.4 8.0 %reduce = bf16[1024,512]{1,0:T(8,128)(2,1)S(1)} reduce(bf16[1024,1,512]{2,1,0:T(2,128)(2,1)} %bitcast.227, bf16[]{:T(256)} %broadcast.491), dimensions={1}, to_apply=%bitcast.213.reduce_sub_computation | reduce | bytes 2097154
  70.1 14.5 %all-to-all-start.1 = ((bf16[32,2,8192]{2,1,0:T(2,128)(2,1)}), bf16[32,2,8192]{2,1,0:T(2,128)(2,1)S(1)}, u32[]{:S(2)}, u32[]{:S(2)}) async-start(bf16[32,2,8192]{2,1,0:T(2,128)(2,1)} %reshape.223), calls=%async_computation.1 | async-start | bytes 2097152 | tf_op jit(solution)/shard_map/all_to_all | solution.py:163
  84.6 16.7 %while.14 = (s32[]{:T(128)}, f32[1024,512]{1,0:T(8,128)S(1)}, f32[512,16]{0,1:T(8,128)S(1)}, f32[512,16]{0,1:T(8,128)S(1)}, s32[]{:T(128)}, /*index=5*/s32[]{:T(128)}, s32[]{:T(128)}) while((s32[]{:T(128)}, f32[1024,512]{1,0:T(8,128)S(1)}, f32[512,16]{0,1:T(8,128)S(1)}, f32[512,16]{0,1:T(8,128)S(1)}, s32[]{:T(128)}, ...), condition=%wide.region_1.2_spmd.clone, body=%wide.region_0.1_spmd.clone.sunk | while | flops 2099715 | bytes 4214887 | solution.py:35
  104.1 8.1 %all-to-all-start.4 = ((f32[1,1024,512]{2,0,1:T(1,128)}), f32[1,1024,512]{2,0,1:T(1,128)}, u32[]{:S(2)}, u32[]{:S(2)}) async-start(f32[1,1024,512]{2,0,1:T(1,128)} %broadcast_in_dim.14), calls=%async_computation.4 | async-start | bytes 4194304 | tf_op jit(solution)/shard_map/all_to_all | solution.py:178
  121.8 15.2 %all-to-all-done.4 = f32[1,1024,512]{2,0,1:T(1,128)} async-done(((f32[1,1024,512]{2,0,1:T(1,128)}), f32[1,1024,512]{2,0,1:T(1,128)}, u32[]{:S(2)}, u32[]{:S(2)}) %all-to-all-start.4) | async-done | bytes 2097184 | tf_op jit(solution)/shard_map/all_to_all | solution.py:178
  143.7 8.5 %add_convert_fusion.1 = (bf16[64,32,512]{2,0,1:T(8,128)(2,1)}, bf16[64,32,512]{2,0,1:T(8,128)(2,1)S(1)}, bf16[64,32,512]{2,0,1:T(8,128)(2,1)}, bf16[64,32,512]{2,0,1:T(8,128)(2,1)}) fusion(f32[64,32,512]{2,0,1:T(8,128)S(1)} %fusion.83, f32[64,32]{0,1:T(8,128)S(1)} %get-tuple-element.166, f32[64,32]{0,1:T(8,128)S(1)} %get-tuple-element.165, ...), kind=kOutput, calls=%fused_computation.38 | convolution fusion | flops 421556224 | bytes 23085056 | tf_op jit(solution)/shard_map/ka,abc->kbc/dot_general | solution.py:47
  154.7 8.7 %all-to-all-start.6 = ((bf16[64,32,512]{2,1,0:T(8,128)(2,1)}), bf16[64,32,512]{2,1,0:T(8,128)(2,1)S(1)}, u32[]{:S(2)}, u32[]{:S(2)}) async-start(bf16[64,32,512]{2,1,0:T(8,128)(2,1)} %copy.152), calls=%async_computation.6 | async-start | bytes 4194304 | tf_op jit(solution)/shard_map/all_to_all | solution.py:184
  167.6 21.6 %all-to-all-done.6 = bf16[64,32,512]{2,1,0:T(8,128)(2,1)S(1)} async-done(((bf16[64,32,512]{2,1,0:T(8,128)(2,1)}), bf16[64,32,512]{2,1,0:T(8,128)(2,1)S(1)}, u32[]{:S(2)}, u32[]{:S(2)}) %all-to-all-start.6) | async-done | bytes 2097184 | tf_op jit(solution)/shard_map/all_to_all | solution.py:184
  189.1 8.0 %all-to-all-start.3 = ((bf16[64,32,512]{2,1,0:T(8,128)(2,1)}), bf16[64,32,512]{2,1,0:T(8,128)(2,1)}, u32[]{:S(2)}, u32[]{:S(2)}) async-start(bf16[64,32,512]{2,1,0:T(8,128)(2,1)} %copy.142), calls=%async_computation.3 | async-start | bytes 4194304 | tf_op jit(solution)/shard_map/all_to_all | solution.py:169
  201.2 21.6 %all-to-all-done.3 = bf16[64,32,512]{2,1,0:T(8,128)(2,1)} async-done(((bf16[64,32,512]{2,1,0:T(8,128)(2,1)}), bf16[64,32,512]{2,1,0:T(8,128)(2,1)}, u32[]{:S(2)}, u32[]{:S(2)}) %all-to-all-start.3) | async-done | bytes 2097184 | tf_op jit(solution)/shard_map/all_to_all | solution.py:169
  222.8 8.0 %all-to-all-start.2 = ((bf16[64,32,512]{2,1,0:T(8,128)(2,1)}), bf16[64,32,512]{2,1,0:T(8,128)(2,1)}, u32[]{:S(2)}, u32[]{:S(2)}) async-start(bf16[64,32,512]{2,1,0:T(8,128)(2,1)} %copy.140), calls=%async_computation.2 | async-start | bytes 4194304 | tf_op jit(solution)/shard_map/all_to_all | solution.py:166
  234.8 21.6 %all-to-all-done.2 = bf16[64,32,512]{2,1,0:T(8,128)(2,1)} async-done(((bf16[64,32,512]{2,1,0:T(8,128)(2,1)}), bf16[64,32,512]{2,1,0:T(8,128)(2,1)}, u32[]{:S(2)}, u32[]{:S(2)}) %all-to-all-start.2) | async-done | bytes 2097184 | tf_op jit(solution)/shard_map/all_to_all | solution.py:166
  256.5 8.4 %all-to-all-start.5 = ((bf16[64,32,512]{2,1,0:T(8,128)(2,1)}), bf16[64,32,512]{2,1,0:T(8,128)(2,1)}, u32[]{:S(2)}, u32[]{:S(2)}) async-start(bf16[64,32,512]{2,1,0:T(8,128)(2,1)} %copy.150), calls=%async_computation.5 | async-start | bytes 4194304 | tf_op jit(solution)/shard_map/all_to_all | solution.py:181
  302.3 11.6 %fusion.12 = (f32[2,32,32,512]{3,1,2,0:T(8,128)S(1)}, f32[2,32,32,512]{3,1,2,0:T(8,128)}, f32[2,32,32,512]{3,1,2,0:T(8,128)S(1)}, f32[2,32,32,512]{3,1,2,0:T(8,128)S(1)}) fusion(f32[2,32,512,32]{2,3,1,0:T(8,128)} %convolution_add_fusion, f32[32,32]{0,1:T(8,128)S(1)} %copy.145, f32[32,32]{0,1:T(8,128)S(1)} %copy.144, ...), kind=kOutput, calls=%fused_computation.21 | convolution fusion | flops 416299008 | bytes 35659776 | tf_op jit(solution)/shard_map/jp,kpqc->kjqc/dot_general | solution.py:67
  313.9 9.0 %fusion.24 = f32[2,32,512,32]{2,3,1,0:T(8,128)S(1)} fusion(f32[2,32,32,512]{3,1,2,0:T(8,128)} %get-tuple-element.138), kind=kOutput, calls=%fused_computation.49 | convolution fusion | flops 402667520 | bytes 8388608 | tf_op jit(solution)/shard_map/mq,kjqc->kmjc/dot_general | solution.py:83
  344.2 7.7 %fusion.46 = f32[2,32,512,32]{2,3,1,0:T(8,128)S(1)} fusion(f32[2,32,512,32]{2,3,1,0:T(8,128)S(1)} %fusion.26, f32[2,32,32,512]{3,1,2,0:T(8,128)S(1)} %get-tuple-element.137), kind=kOutput, calls=%fused_computation.67 | convolution fusion | flops 403716096 | bytes 12582912 | tf_op jit(solution)/shard_map/mq,kjqc->kmjc/dot_general | solution.py:80
  351.9 7.4 %fusion.49 = f32[2,32,512,32]{2,3,1,0:T(8,128)} fusion(f32[2,32,512,32]{2,3,1,0:T(8,128)S(1)} %fusion.24, f32[2,32,32,512]{3,1,2,0:T(8,128)S(1)} %get-tuple-element.137), kind=kOutput, calls=%fused_computation.68 | convolution fusion | flops 403716096 | bytes 12582912 | tf_op jit(solution)/shard_map/mq,kjqc->kmjc/dot_general | solution.py:83
  359.3 7.6 %fusion.40 = f32[2,32,512,32]{2,3,1,0:T(8,128)} fusion(f32[2,32,512,32]{2,3,1,0:T(8,128)S(1)} %fusion.34, f32[2,32,32,512]{3,1,2,0:T(8,128)S(1)} %get-tuple-element.160), kind=kOutput, calls=%fused_computation.65 | convolution fusion | flops 403716096 | bytes 12582912 | tf_op jit(solution)/shard_map/mq,kjqc->kmjc/dot_general | solution.py:80
  366.9 10.6 %multiply_subtract_fusion = (f32[2,32,512,32]{2,3,1,0:T(8,128)S(1)}, f32[2,32,512,32]{2,3,1,0:T(8,128)S(1)}) fusion(f32[2,32,512,32]{2,3,1,0:T(8,128)} %fusion.49, f32[2,32,512,32]{2,3,1,0:T(8,128)} %fusion.40, f32[2,32,512,32]{2,3,1,0:T(8,128)S(1)} %fusion.46, f32[2,32,512,32]{2,3,1,0:T(8,128)} %fusion.32, f32[2,32,32,512]{3,1,2,0:T(8,128)S(1)} %get-tuple-element.160), kind=kOutput, calls=%fused_computation.36 | convolution fusion | flops 410007552 | bytes 29360128 | tf_op jit(solution)/shard_map/mq,kjqc->kmjc/dot_general | solution.py:83
  398.1 7.4 %fusion.16 = f32[2,32,512,32]{2,3,1,0:T(8,128)S(1)} fusion(f32[2,32,32,512]{3,2,1,0:T(8,128)S(1)} %get-tuple-element.136), kind=kOutput, calls=%fused_computation.41 | convolution fusion | flops 402667520 | bytes 8388608 | tf_op jit(solution)/shard_map/pj,kjqc->kpqc/dot_general | solution.py:114
  412.5 7.9 %subtract_bitcast_fusion = f32[2,32,32,512]{3,1,2,0:T(8,128)S(1)} fusion(f32[2,32,512,32]{2,3,1,0:T(8,128)S(1)} %fusion.18, f32[2,32,32,512]{3,2,1,0:T(8,128)S(1)} %get-tuple-element.135), kind=kOutput, calls=%fused_computation.32 | convolution fusion | flops 403716096 | bytes 12582912 | tf_op jit(solution)/shard_map/pj,kjqc->kpqc/dot_general | solution.py:111
  420.3 7.5 %add_bitcast_fusion = f32[2,32,32,512]{3,1,2,0:T(8,128)S(1)} fusion(f32[2,32,512,32]{2,3,1,0:T(8,128)S(1)} %fusion.16, f32[2,32,32,512]{3,2,1,0:T(8,128)S(1)} %get-tuple-element.135), kind=kOutput, calls=%fused_computation.31 | convolution fusion | flops 403716096 | bytes 12582912 | tf_op jit(solution)/shard_map/pj,kjqc->kpqc/dot_general | solution.py:114
  441.2 7.8 %all-to-all-start.8 = ((f32[2,1024,512]{2,0,1:T(2,128)}), f32[2,1024,512]{2,0,1:T(2,128)}, u32[]{:S(2)}, u32[]{:S(2)}) async-start(f32[2,1024,512]{2,0,1:T(2,128)} %copy.169), calls=%async_computation.8 | async-start | bytes 8388608 | tf_op jit(solution)/shard_map/all_to_all | solution.py:194
  449.0 7.4 %copy.166 = f32[2,1024,512]{2,0,1:T(2,128)} copy(f32[2,1024,512]{2,1,0:T(8,128)} %get-tuple-element.146) | data formatting | bytes 8388608 | tf_op jit(solution)/shard_map/sub | solution.py:126
  456.4 41.0 %all-to-all-done.8 = f32[2,1024,512]{2,0,1:T(2,128)} async-done(((f32[2,1024,512]{2,0,1:T(2,128)}), f32[2,1024,512]{2,0,1:T(2,128)}, u32[]{:S(2)}, u32[]{:S(2)}) %all-to-all-start.8) | async-done | bytes 4194336 | tf_op jit(solution)/shard_map/all_to_all | solution.py:194
  497.4 11.5 %all-to-all-start.7 = ((f32[2,1024,512]{2,0,1:T(2,128)}), f32[2,1024,512]{2,0,1:T(2,128)}, u32[]{:S(2)}, u32[]{:S(2)}) async-start(f32[2,1024,512]{2,0,1:T(2,128)} %copy.166), calls=%async_computation.7 | async-start | bytes 8388608 | tf_op jit(solution)/shard_map/all_to_all | solution.py:193
  523.3 39.2 %all-to-all-done.7 = f32[2,1024,512]{2,0,1:T(2,128)} async-done(((f32[2,1024,512]{2,0,1:T(2,128)}), f32[2,1024,512]{2,0,1:T(2,128)}, u32[]{:S(2)}, u32[]{:S(2)}) %all-to-all-start.7) | async-done | bytes 4194336 | tf_op jit(solution)/shard_map/all_to_all | solution.py:193
  584.1 21.9 %all_to_all.164 = bf16[32,32,512]{2,1,0:T(8,128)(2,1)} all-to-all(bf16[32,32,512]{2,1,0:T(8,128)(2,1)S(1)} %copy.172), channel_id=1, replica_groups=mesh['seq'=32,'ch'=8] {'seq'}, dimensions={0} | all-to-all | bytes 2097152 | tf_op jit(solution)/shard_map/all_to_all | solution.py:197
  606.0 7.4 %all-to-all-start.10 = ((bf16[8,128,512]{2,1,0:T(8,128)(2,1)}), bf16[8,128,512]{2,1,0:T(8,128)(2,1)S(1)}, u32[]{:S(2)}, u32[]{:S(2)}) async-start(bf16[8,128,512]{2,1,0:T(8,128)(2,1)} %bitcast.52), calls=%async_computation.10 | async-start | bytes 2097152 | tf_op jit(solution)/shard_map/all_to_all | solution.py:198
  618.6 16.9 %all-to-all-done.10 = bf16[8,128,512]{2,1,0:T(8,128)(2,1)S(1)} async-done(((bf16[8,128,512]{2,1,0:T(8,128)(2,1)}), bf16[8,128,512]{2,1,0:T(8,128)(2,1)S(1)}, u32[]{:S(2)}, u32[]{:S(2)}) %all-to-all-start.10) | async-done | bytes 1048608 | tf_op jit(solution)/shard_map/all_to_all | solution.py:198
  (149 shorter events, 227.4 us)
Async XLA Ops:
  1.9 11.5 %collective-permute-start = (bf16[3,2,4096]{2,1,0:T(2,128)(2,1)S(1)}, bf16[3,2,4096]{2,1,0:T(2,128)(2,1)S(1)}, u32[]{:S(2)}, u32[]{:S(2)}) collective-permute-start(bf16[3,2,4096]{2,1,0:T(2,128)(2,1)S(1)} %pad_maximum_fusion), channel_id=1, source_target_pairs={{0,1},{1,2},{2,3},{3,4},{4,5},{5,6},{6,7},{7,8},{8,9},{9,10},{10,1... | collective-permute-start | bytes 147464 | tf_op jit(solution)/shard_map/ppermute | solution.py:15
  18.7 14.3 %copy-start.10 = (f32[512,16]{0,1:T(8,128)S(1)}, f32[512,16]{0,1:T(8,128)}, u32[]{:S(2)}) copy-start(f32[512,16]{0,1:T(8,128)} %param.13) | copy-start | bytes 98308
  18.7 14.3 %copy-start.11 = (f32[512,16]{0,1:T(8,128)S(1)}, f32[512,16]{0,1:T(8,128)}, u32[]{:S(2)}) copy-start(f32[512,16]{0,1:T(8,128)} %param.14) | copy-start | bytes 98308
  25.7 28.8 %all-to-all-start = ((bf16[128,8,512]{0,2,1:T(8,128)(2,1)}), bf16[128,8,512]{0,2,1:T(8,128)(2,1)S(1)}, u32[]{:S(2)}, u32[]{:S(2)}) async-start(bf16[128,8,512]{0,2,1:T(8,128)(2,1)} %bitcast.17), calls=%async_computation | async-start | bytes 2097152 | tf_op jit(solution)/shard_map/all_to_all | solution.py:156
  54.5 1.0 copy-start.4
  70.1 34.1 %all-to-all-start.1 = ((bf16[32,2,8192]{2,1,0:T(2,128)(2,1)}), bf16[32,2,8192]{2,1,0:T(2,128)(2,1)S(1)}, u32[]{:S(2)}, u32[]{:S(2)}) async-start(bf16[32,2,8192]{2,1,0:T(2,128)(2,1)} %reshape.223), calls=%async_computation.1 | async-start | bytes 2097152 | tf_op jit(solution)/shard_map/all_to_all | solution.py:163
  104.1 32.8 %all-to-all-start.4 = ((f32[1,1024,512]{2,0,1:T(1,128)}), f32[1,1024,512]{2,0,1:T(1,128)}, u32[]{:S(2)}, u32[]{:S(2)}) async-start(f32[1,1024,512]{2,0,1:T(1,128)} %broadcast_in_dim.14), calls=%async_computation.4 | async-start | bytes 4194304 | tf_op jit(solution)/shard_map/all_to_all | solution.py:178
  137.0 6.7 %copy-start.3 = (f32[64,32,512]{2,0,1:T(8,128)S(1)}, f32[64,32,512]{2,0,1:T(8,128)}, u32[]{:S(2)}) copy-start(f32[64,32,512]{2,0,1:T(8,128)} %fusion.97) | copy-start | bytes 12582916
  138.9 4.8 copy-start.2
  154.7 34.4 %all-to-all-start.6 = ((bf16[64,32,512]{2,1,0:T(8,128)(2,1)}), bf16[64,32,512]{2,1,0:T(8,128)(2,1)S(1)}, u32[]{:S(2)}, u32[]{:S(2)}) async-start(bf16[64,32,512]{2,1,0:T(8,128)(2,1)} %copy.152), calls=%async_computation.6 | async-start | bytes 4194304 | tf_op jit(solution)/shard_map/all_to_all | solution.py:184
  189.1 33.7 %all-to-all-start.3 = ((bf16[64,32,512]{2,1,0:T(8,128)(2,1)}), bf16[64,32,512]{2,1,0:T(8,128)(2,1)}, u32[]{:S(2)}, u32[]{:S(2)}) async-start(bf16[64,32,512]{2,1,0:T(8,128)(2,1)} %copy.142), calls=%async_computation.3 | async-start | bytes 4194304 | tf_op jit(solution)/shard_map/all_to_all | solution.py:169
  222.8 33.7 %all-to-all-start.2 = ((bf16[64,32,512]{2,1,0:T(8,128)(2,1)}), bf16[64,32,512]{2,1,0:T(8,128)(2,1)}, u32[]{:S(2)}, u32[]{:S(2)}) async-start(bf16[64,32,512]{2,1,0:T(8,128)(2,1)} %copy.140), calls=%async_computation.2 | async-start | bytes 4194304 | tf_op jit(solution)/shard_map/all_to_all | solution.py:166
  256.5 36.3 %all-to-all-start.5 = ((bf16[64,32,512]{2,1,0:T(8,128)(2,1)}), bf16[64,32,512]{2,1,0:T(8,128)(2,1)}, u32[]{:S(2)}, u32[]{:S(2)}) async-start(bf16[64,32,512]{2,1,0:T(8,128)(2,1)} %copy.150), calls=%async_computation.5 | async-start | bytes 4194304 | tf_op jit(solution)/shard_map/all_to_all | solution.py:181
  313.9 9.0 %copy-start = (f32[2,32,32,512]{3,1,2,0:T(8,128)S(1)}, f32[2,32,32,512]{3,1,2,0:T(8,128)}, u32[]{:S(2)}) copy-start(f32[2,32,32,512]{3,1,2,0:T(8,128)} %get-tuple-element.138) | copy-start | bytes 12582916
  441.2 56.3 %all-to-all-start.8 = ((f32[2,1024,512]{2,0,1:T(2,128)}), f32[2,1024,512]{2,0,1:T(2,128)}, u32[]{:S(2)}, u32[]{:S(2)}) async-start(f32[2,1024,512]{2,0,1:T(2,128)} %copy.169), calls=%async_computation.8 | async-start | bytes 8388608 | tf_op jit(solution)/shard_map/all_to_all | solution.py:194
  497.4 65.0 %all-to-all-start.7 = ((f32[2,1024,512]{2,0,1:T(2,128)}), f32[2,1024,512]{2,0,1:T(2,128)}, u32[]{:S(2)}, u32[]{:S(2)}) async-start(f32[2,1024,512]{2,0,1:T(2,128)} %copy.166), calls=%async_computation.7 | async-start | bytes 8388608 | tf_op jit(solution)/shard_map/all_to_all | solution.py:193
  576.7 4.4 copy-start.1
  583.5 29.8 %copy-start.5 = (bf16[128,4096]{1,0:T(8,128)(2,1)S(1)}, bf16[128,4096]{1,0:T(8,128)(2,1)}, u32[]{:S(2)}) copy-start(bf16[128,4096]{1,0:T(8,128)(2,1)} %param.9) | copy-start | bytes 3145732
  583.5 30.5 %copy-start.9 = (bf16[1,2,4096]{2,1,0:T(2,128)(2,1)S(1)}, bf16[1,2,4096]{2,1,0:T(2,128)(2,1)}, u32[]{:S(2)}) copy-start(bf16[1,2,4096]{2,1,0:T(2,128)(2,1)} %get-tuple-element.156) | copy-start | bytes 49156
  606.0 29.5 %all-to-all-start.10 = ((bf16[8,128,512]{2,1,0:T(8,128)(2,1)}), bf16[8,128,512]{2,1,0:T(8,128)(2,1)S(1)}, u32[]{:S(2)}, u32[]{:S(2)}) async-start(bf16[8,128,512]{2,1,0:T(8,128)(2,1)} %bitcast.52), calls=%async_computation.10 | async-start | bytes 2097152 | tf_op jit(solution)/shard_map/all_to_all | solution.py:198
  614.0 1.3 copy-start.6
  614.0 1.3 copy-start.7
  614.0 1.3 copy-start.8
  615.4 20.8 %copy-start.12 = (f32[4096]{0:T(1024)S(1)}, f32[4096]{0:T(1024)}, u32[]{:S(2)}) copy-start(f32[4096]{0:T(1024)} %param.15) | copy-start | bytes 49156
where the time goes:
time: 650 us; the launch traced here: 640 us
  waiting for transfers between devices  199 us (31%)
  matrix products  190 us (29%)
  starting transfers between devices  96 us (15%)
  local copies, waits for them, and re-layouts  88 us (14%)
  other arithmetic  43.2 us (7%)
  blocking collectives  21.9 us (3%)
    all_to_all x1, waiting for transfers between devices, on_device(): lax.all_to_all(back_im, 'seq', split_axis=1, concat_axis=0, tiled=True)  41 us
    all_to_all x1, waiting for transfers between devices, on_device(): lax.all_to_all(back_re, 'seq', split_axis=1, concat_axis=0, tiled=True)  39.2 us
    all_to_all x1, blocking collectives, on_device(): lax.all_to_all(conv_rows, 'seq', split_axis=0, concat_axis=1, tiled=True)[0]  21.9 us
    all_to_all x1, waiting for transfers between devices, on_device(): lax.all_to_all(sig_re.astype(jnp.bfloat16), 'seq', split_axis=0, concat_a...  21.6 us
    all_to_all x1, waiting for transfers between devices, on_device(): lax.all_to_all(sig_im.astype(jnp.bfloat16), 'seq', split_axis=0, concat_a...  21.6 us
    all_to_all x1, waiting for transfers between devices, on_device(): lax.all_to_all(fil_im.astype(jnp.bfloat16), 'seq', split_axis=0, concat_a...  21.6 us
    all_to_all x1, waiting for transfers between devices, on_device(): lax.all_to_all(signal, 'ch', split_axis=1, concat_axis=0, tiled=True)  21.4 us
    dot_general x2, matrix products, columns_forward(): jnp.einsum('jp,kpqc->kjqc', sin_p, real, precision=HIGHEST)  18.6 us
  transfers between devices with their start and end apart: 11, of which 8 were waited for; matrix products, arithmetic and copies ran while one was open for 15% of the time, Pallas kernels for 0%

commit v1 on v0

v1 whole, which is shorter than its diff:
```python
import functools
import math

import jax
import jax.numpy as jnp
import numpy as np
from jax import lax
from jax.experimental import pallas as pl
from jax.experimental.pallas import tpu as pltpu
from jax.sharding import PartitionSpec as P

F32, BF16 = jnp.float32, jnp.bfloat16
HIGHEST = lax.Precision.HIGHEST
NX, NY, NZ, NH = 4, 4, 2, 4
SPEC = pltpu.PrefetchScalarGridSpec


def transforms(rows):
    k = np.arange(rows)[:, None]
    n = np.arange(rows)[None, :]
    angle = np.pi * (((2 * k + 1) * n) % (4 * rows)) / (2 * rows)
    forward = np.concatenate([np.cos(angle), -np.sin(angle)], axis=0)
    inverse = np.concatenate([np.cos(angle).T, -np.sin(angle).T], axis=1) / rows
    return forward.astype(np.float32), inverse.astype(np.float32)


def rounded(value):
    return value.astype(BF16).astype(F32)


def mix(now, one, two, taps):
    return taps[0:1] * now + taps[1:2] * one + taps[2:3] * two


def mix_block(block, taps):
    return mix(block, pltpu.roll(block, 1, 0), pltpu.roll(block, 2, 0), taps)


def mix_top(block, edge, taps):
    a, b = block[0:1], block[1:2]
    e0, e1 = edge[0:1], edge[1:2]
    return mix(a, e1, e0, taps), mix(b, a, e1, taps)


def signal_kernel(k_ref, v_ref, filt_ref, sig_ref):
    key = mix_block(k_ref[...].astype(F32), filt_ref[1])
    value = mix_block(v_ref[...].astype(F32), filt_ref[2])
    sig_ref[...] = rounded(key * value)


def signal_call(k_proj, v_proj, filt, group):
    rows, width = k_proj.shape
    block = pl.BlockSpec((rows, group), lambda g: (0, g))
    return pl.pallas_call(
        signal_kernel,
        grid=(width // group,),
        in_specs=[block, block, pl.BlockSpec((3, 3, group), lambda g: (0, 0, g))],
        out_specs=block,
        out_shape=jax.ShapeDtypeStruct((rows, width), F32),
        cost_estimate=pl.CostEstimate(flops=rows * width * 12, bytes_accessed=rows * width * 8, transcendentals=0),
    )(k_proj, v_proj, filt)


def lane_group(flip):
    def group(k, place):
        return (place[0] + NH - k) % NH * 2 + (place[1] + flip) % 2

    return group


def state_kernel(place, rate_ref, sig_ref, k_ref, v_ref, edge_ref, filt_ref, state_ref, top_ref):
    rows = sig_ref.shape[0]
    half = rows // 2
    decay = jnp.exp(-rate_ref[0])
    edges = edge_ref[...].astype(F32)
    key = mix_top(k_ref[...].astype(F32), edges[1], filt_ref[1])
    value = mix_top(v_ref[...].astype(F32), edges[2], filt_ref[2])
    s0, s1 = rounded(key[0] * value[0]), rounded(key[1] * value[1])
    row = lax.broadcasted_iota(jnp.int32, top_ref.shape, 0)
    top_ref[...] = jnp.where(row == 0, s0, jnp.where(row == 1, s1, sig_ref[0:8, :]))
    early = s0 * decay + s1
    late = sig_ref[half : half + 1, :] * decay + sig_ref[half + 1 : half + 2, :]
    for t in range(2, half):
        early = early * decay + sig_ref[t : t + 1, :]
        late = late * decay + sig_ref[half + t : half + t + 1, :]
    state_ref[0] = early * jnp.exp(-rate_ref[0] * half) + late


def state_call(place, rates, sig, k_proj, v_proj, edges, filt, flip):
    rows, width = sig.shape
    modes, group = rates.shape[1:]
    at = lane_group(flip)
    return pl.pallas_call(
        state_kernel,
        grid_spec=SPEC(
            num_scalar_prefetch=1,
            grid=(NH,),
            in_specs=[
                pl.BlockSpec((1, modes, group), lambda k, p: (k, 0, 0)),
                pl.BlockSpec((rows, group), lambda k, p: (0, at(k, p))),
                pl.BlockSpec((16, group), lambda k, p: (0, at(k, p))),
                pl.BlockSpec((16, group), lambda k, p: (0, at(k, p))),
                pl.BlockSpec((3, 2, group), lambda k, p: (0, 0, at(k, p))),
                pl.BlockSpec((3, 3, group), lambda k, p: (0, 0, at(k, p))),
            ],
            out_specs=[
                pl.BlockSpec((1, modes, group), lambda k, p: (k, 0, 0)),
                pl.BlockSpec((8, group), lambda k, p: (0, at(k, p))),
            ],
        ),
        out_shape=[
            jax.ShapeDtypeStruct((NH, modes, group), F32),
            jax.ShapeDtypeStruct((rows, width), F32),
        ],
        input_output_aliases={2: 1},
        cost_estimate=pl.CostEstimate(
            flops=rows * width * modes, bytes_accessed=rows * width * 2, transcendentals=0
        ),
    )(place, rates, sig, k_proj, v_proj, edges, filt)


def local_kernel(place, chunk, rate0, rate1, weight0, weight1, sig_ref, q_ref, edge_ref, filt_ref,
                 fwd_ref, inv_ref, _, __, conv_ref, query_ref, taps_ref, rate_s, step_s, weight_s):
    own = (pl.program_id(0) + place[1]) % 2 == 0
    rows, group = sig_ref.shape
    modes = rate_s.shape[0]
    rate_s[...] = jnp.where(own, rate0[0], rate1[0])
    weight_s[...] = jnp.where(own, weight0[0], weight1[0])
    step_s[...] = jnp.exp(-8.0 * rate_s[...])
    ramp = lax.broadcasted_iota(jnp.int32, (8, 128), 0).astype(F32)

    for lane in range(0, group, 128):
        at = slice(lane, lane + 128)
        terms = [
            weight_s[m : m + 1, at] * jnp.exp(-rate_s[m : m + 1, at] * ramp) for m in range(modes)
        ]
        steps = [jnp.broadcast_to(step_s[m : m + 1, at], (8, 128)) for m in range(modes)]
        for tile in range(rows // 8):
            total = functools.reduce(lambda a, b: a + b, terms)
            taps_ref[tile * 8 : tile * 8 + 8, at] = total
            if tile + 1 < rows // 8:
                terms = [a * b for a, b in zip(terms, steps)]

    fwd = fwd_ref[...]
    sig = jnp.dot(fwd, sig_ref[...], precision=HIGHEST, preferred_element_type=F32)
    fil = jnp.dot(fwd, taps_ref[...], precision=HIGHEST, preferred_element_type=F32)
    sr, si, fr, fi = sig[:rows], sig[rows:], fil[:rows], fil[rows:]
    prod = jnp.concatenate([sr * fr - si * fi, sr * fi + si * fr], axis=0)
    conv_ref[...] = jnp.dot(inv_ref[...], prod, precision=HIGHEST, preferred_element_type=F32)

    q = q_ref[...].astype(F32)
    query = mix_block(q, filt_ref[0])
    q0, q1 = mix_top(q, edge_ref[0].astype(F32), filt_ref[0])
    row = lax.broadcasted_iota(jnp.int32, query.shape, 0)
    query_ref[...] = jnp.where(row == 0, q0, jnp.where(row == 1, q1, query)).astype(BF16)


def local_call(place, chunk, rates, weights, sig, q_proj, edges, filt, before):
    rows, width = sig.shape
    modes, group = rates[0].shape[1:]
    fwd, inv = transforms(rows)

    def par(n, p):
        return ((p[0] + NH - chunk) % NH, 0, 0)

    def lanes(n, p):
        return (0, 2 * chunk + n)

    def lanes3(n, p):
        return (0, 0, 2 * chunk + n)

    par_spec = pl.BlockSpec((1, modes, group), par)
    any_spec = pl.BlockSpec(memory_space=pl.ANY)
    body = functools.partial(local_kernel)
    shapes = [jax.ShapeDtypeStruct((rows, width), F32), jax.ShapeDtypeStruct((rows, width), BF16)]

    def kernel(p, r0, r1, w0, w1, s, q, e, f, a, b, *rest):
        if before is None:
            rest = (None, None) + rest
        body(p, chunk, r0, r1, w0, w1, s, q, e, f, a, b, *rest)

    return pl.pallas_call(
        kernel,
        grid_spec=SPEC(
            num_scalar_prefetch=1,
            grid=(2,),
            in_specs=[par_spec] * 4
            + [
                pl.BlockSpec((rows, group), lanes),
                pl.BlockSpec((rows, group), lanes),
                pl.BlockSpec((3, 2, group), lanes3),
                pl.BlockSpec((3, 3, group), lanes3),
                pl.BlockSpec((2 * rows, rows), lambda n, p: (0, 0)),
                pl.BlockSpec((rows, 2 * rows), lambda n, p: (0, 0)),
            ]
            + ([] if before is None else [any_spec, any_spec]),
            out_specs=[pl.BlockSpec((rows, group), lanes), pl.BlockSpec((rows, group), lanes)],
            scratch_shapes=[
                pltpu.VMEM((rows, group), F32),
                pltpu.VMEM((modes, group), F32),
                pltpu.VMEM((modes, group), F32),
                pltpu.VMEM((modes, group), F32),
            ],
        ),
        out_shape=shapes,
        input_output_aliases={} if before is None else {11: 0, 12: 1},
        cost_estimate=pl.CostEstimate(
            flops=rows * width * modes, bytes_accessed=rows * width * 4, transcendentals=0
        ),
    )(place, *rates, *weights, sig, q_proj, edges, filt, jnp.asarray(fwd), jnp.asarray(inv), *(before or ()))


def carry_kernel(place, rate_ref, weight_ref, state_ref, conv_ref, query_ref, sig_ref, skip_ref, *rest):
    out_ref, start_s, step_s, carry_s = rest[-4:]
    rows, group = sig_ref.shape
    modes = rate_ref.shape[1]
    start_s[...] = weight_ref[0] * state_ref[0]
    step_s[...] = jnp.exp(-8.0 * rate_ref[0])
    ramp = lax.broadcasted_iota(jnp.int32, (8, 128), 0).astype(F32) + 1.0
    for lane in range(0, group, 128):
        at = slice(lane, lane + 128)
        terms = [
            start_s[m : m + 1, at] * jnp.exp(-rate_ref[0, m : m + 1, at] * ramp)
            for m in range(modes)
        ]
        steps = [jnp.broadcast_to(step_s[m : m + 1, at], (8, 128)) for m in range(modes)]
        for tile in range(rows // 8):
            total = functools.reduce(lambda a, b: a + b, terms)
            carry_s[tile * 8 : tile * 8 + 8, at] = total
            if tile + 1 < rows // 8:
                terms = [a * b for a, b in zip(terms, steps)]
    conv = rounded(conv_ref[...] + carry_s[...])
    out_ref[...] = (query_ref[...].astype(F32) * (conv + skip_ref[...] * sig_ref[...])).astype(BF16)


def carry_call(place, rates, weights, states, conv, query, sig, skip, flip, before):
    rows, width = sig.shape
    modes, group = rates.shape[1:]
    at = lane_group(flip)
    par = pl.BlockSpec((1, modes, group), lambda k, p: (k, 0, 0))
    block = pl.BlockSpec((rows, group), lambda k, p: (0, at(k, p)))
    return pl.pallas_call(
        carry_kernel,
        grid_spec=SPEC(
            num_scalar_prefetch=1,
            grid=(NH,),
            in_specs=[par, par, par, block, block, block, pl.BlockSpec((1, group), lambda k, p: (0, at(k, p)))]
            + ([] if before is None else [pl.BlockSpec(memory_space=pl.ANY)]),
            out_specs=block,
            scratch_shapes=[
                pltpu.VMEM((modes, group), F32),
                pltpu.VMEM((modes, group), F32),
                pltpu.VMEM((rows, group), F32),
            ],
        ),
        out_shape=jax.ShapeDtypeStruct((rows, width), BF16),
        input_output_aliases={} if before is None else {8: 0},
        cost_estimate=pl.CostEstimate(
            flops=rows * width * modes, bytes_accessed=rows * width * 4, transcendentals=0
        ),
    )(place, rates, weights, states, conv, query, sig, skip, *(() if before is None else (before,)))


def moved(value, axis, target):
    return lax.ppermute(value, axis, [(i, target(i)) for i in range(lax.axis_size(axis))])


def to_chip(value, by):
    return moved(value, "ch", lambda i: (i + 2 * by) % (2 * NH))


def to_core(value):
    return moved(value, "ch", lambda i: i ^ 1)


def to_x(value, by):
    return moved(value, "seq", lambda i: i // NX * NX + (i + by) % NX)


def to_y(value, by):
    span = NX * NY
    return moved(value, "seq", lambda i: i // span * span + (i + by * NX) % span)


def to_z(value):
    return moved(value, "seq", lambda i: (i + NX * NY) % (NX * NY * NZ))


def power(rates, count):
    return jnp.exp(-rates * jnp.asarray(count, F32))


def prefix(values, place, rates, span):
    size = len(values)
    start = jnp.zeros_like(values[0])
    end = jnp.zeros_like(values[0])
    for n, value in enumerate(values):
        source = (place - n) % size
        end += value * power(rates, span * (size - 1 - source))
        if n:
            start += jnp.where(n <= place, value * power(rates, span * (n - 1)), 0.0)
    return start, end


def on_device(q_proj, k_proj, v_proj, short_filter, rates, residues, skip):
    rows, width = q_proj.shape
    seq_at, ch_at = lax.axis_index("seq"), lax.axis_index("ch")
    x_at, y_at, z_at = seq_at % NX, seq_at // NX % NY, seq_at // (NX * NY)
    h_at, core = ch_at // 2, ch_at % 2
    place = jnp.stack([h_at, core]).astype(jnp.int32)
    group = rates.shape[0]

    edges = jnp.stack([q_proj[-2:], k_proj[-2:], v_proj[-2:]])
    total = lax.axis_size(("seq", "ch"))
    edges = lax.ppermute(edges, ("seq", "ch"), [(i, i + 1) for i in range(total - 1)])

    own_rates = rates.T
    rates0 = jnp.stack([own_rates] + [to_chip(own_rates, k) for k in range(1, NH)])
    rates1 = to_core(rates0)
    own_weights = (residues * jnp.sqrt(-jnp.expm1(-2.0 * rates))).T
    weights0 = jnp.stack([own_weights] + [to_chip(own_weights, k) for k in range(1, NH)])
    weights1 = to_core(weights0)

    sig = signal_call(k_proj, v_proj, short_filter, group)
    state0, sig = state_call(place, rates0, sig, k_proj, v_proj, edges, short_filter, 0)
    state1, sig = state_call(place, rates1, sig, k_proj, v_proj, edges, short_filter, 1)

    other1 = to_core(state0)
    first = jnp.where(core == 0, state1, other1)
    second = jnp.where(core == 0, other1, state1)
    chip = first * power(rates1, rows) + second

    mine = rates1[0]
    got = [chip[0]] + [to_chip(chip[k], -k) for k in range(1, NH)]
    whole = jnp.zeros_like(mine)
    starts = [jnp.zeros_like(mine) for _ in range(NH)]
    for k in range(NH):
        source = (h_at + k) % NH
        whole += got[k] * power(mine, 2 * rows * (NH - 1 - source))
        for j in range(NH):
            target = (h_at + j) % NH
            weight = power(mine, 2 * rows * jnp.maximum(target - 1 - source, 0))
            starts[j] += jnp.where(source < target, got[k] * weight, 0.0)

    span = 2 * NH * rows
    before_x, row = prefix([whole] + [to_x(whole, n) for n in range(1, NX)], x_at, mine, span)
    before_y, plane = prefix([row] + [to_y(row, n) for n in range(1, NY)], y_at, mine, span * NX)
    before_z = jnp.where(z_at == 1, to_z(plane), 0.0)
    start = before_x + power(mine, span * x_at) * (
        before_y + power(mine, span * NX * y_at) * before_z
    )
    sent = []
    for j in range(NH):
        target = (h_at + j) % NH
        sent.append(starts[j] + power(mine, 2 * rows * target) * start)
    carry = jnp.stack([sent[0]] + [to_chip(sent[j], j) for j in range(1, NH)])
    later = first + power(rates1, rows) * carry
    carry1 = jnp.where(core == 0, carry, later)
    carry0 = to_core(jnp.where(core == 0, later, carry))

    bufs = None
    for chunk in range(NH):
        bufs = local_call(
            place, chunk, (rates0, rates1), (weights0, weights1), sig, q_proj, edges, short_filter, bufs
        )
    conv, query = bufs

    skip = skip[None, :]
    out = carry_call(place, rates1, weights1, carry1, conv, query, sig, skip, 1, None)
    return carry_call(place, rates0, weights0, carry0, conv, query, sig, skip, 0, out)


def solution(mesh):
    placed = (
        P(("seq", "ch"), None),
        P(("seq", "ch"), None),
        P(("seq", "ch"), None),
        P(),
        P("ch", None),
        P("ch", None),
        P(),
    )
    return jax.shard_map(
        on_device, mesh=mesh, in_specs=placed, out_specs=P(("seq", "ch"), None), check_vma=False
    )
```

time: 650 us -> 128 us (0.20); the launches traced: 640 us -> 127 us
  matrix products: 190 us -> 0 us
  waiting for transfers between devices: 199 us -> 12 us
  local copies, waits for them, and re-layouts: 88 us -> 4.9 us
  Pallas kernels: 0 us -> 51.4 us
  starting transfers between devices: 96 us -> 52.5 us
  other arithmetic: 43.2 us -> 5.86 us
  blocking collectives: 21.9 us -> 0 us
    all_to_all x10 -> x0, waiting for transfers between devices: 199 us -> none  [the longest x1 41 us: on_device(): lax.all_to_all(back_im, 'seq', split_axis=1, concat_axis=0, tiled=True)]
    dot_general x30 -> x0, matrix products: 190 us -> none  [the longest x2 18.6 us: columns_forward(): jnp.einsum('jp,kpqc->kjqc', sin_p, real, precision=HIGHEST)]
    all_to_all x10 -> x0, starting transfers between devices: 89.7 us -> none  [the longest x1 14.5 us: on_device(): lax.all_to_all(grouped[None], 'seq', split_axis=1, concat_axis=0, tiled=T...]
    pallas_call x0 -> x9, Pallas kernels: none -> 51.4 us  [the longest x4 25.3 us: local_call(): pl.pallas_call(kernel, grid_spec=SPEC(num_scalar_prefetch=1, grid=(2,), i...]
    ppermute x1 -> x24, starting transfers between devices: 6.29 us -> 52.5 us  [the longest x23 49.2 us: moved(): lax.ppermute(value, axis, [(i, target(i)) for i in range(lax.axis_size(ax...]
    all_to_all x8 -> x0, local copies, waits for them, and re-layouts: 30.7 us -> none  [the longest x3 14.3 us: on_device(): lax.all_to_all(back_re, 'seq', split_axis=1, concat_axis=0, tiled=True)]
    all_to_all x1 -> x0, blocking collectives: 21.9 us -> none  [on_device(): lax.all_to_all(conv_rows, 'seq', split_axis=0, concat_axis=1, tiled=True)[0]]
    convert_element_type x6 -> x0, local copies, waits for them, and re-layouts: 16.7 us -> none  [the longest x1 4.14 us: on_device(): sig_im.astype(jnp.bfloat16)]
  transfers between devices with their start and end apart: 11 -> 24, of which waited for: 8 -> 7; matrix products, arithmetic and copies ran while one was open for 15% -> 3% of each run, Pallas kernels for 0% -> 36%
where the time goes in v1:
time: 128 us; the launch traced here: 127 us
  starting transfers between devices  52.5 us (41%)
  Pallas kernels  51.4 us (40%)
  waiting for transfers between devices  12 us (9%)
  other arithmetic  5.86 us (5%)
  local copies, waits for them, and re-layouts  4.9 us (4%)
    ppermute x23, starting transfers between devices, moved(): lax.ppermute(value, axis, [(i, target(i)) for i in range(lax.axis_size(ax...  49.2 us
    pallas_call x4, Pallas kernels, local_call(): pl.pallas_call(kernel, grid_spec=SPEC(num_scalar_prefetch=1, grid=(2,), i...  25.3 us
    ppermute x23, waiting for transfers between devices, moved(): lax.ppermute(value, axis, [(i, target(i)) for i in range(lax.axis_size(ax...  12 us
    pallas_call x2, Pallas kernels, carry_call(): pl.pallas_call(carry_kernel, grid_spec=SPEC(num_scalar_prefetch=1, grid=(...  10.2 us
    pallas_call x2, Pallas kernels, state_call(): pl.pallas_call(state_kernel, grid_spec=SPEC(num_scalar_prefetch=1, grid=(...  9.39 us
    pallas_call x1, Pallas kernels, signal_call(): pl.pallas_call(signal_kernel, grid=(width // group,), in_specs=[block, bl...  6.47 us
    ppermute x1, starting transfers between devices, on_device(): lax.ppermute(edges, ('seq', 'ch'), [(i, i + 1) for i in range(total - 1)])  3.29 us
    unnamed x20, local copies, waits for them, and re-layouts  3.12 us
  transfers between devices with their start and end apart: 24, of which 7 were waited for; matrix products, arithmetic and copies ran while one was open for 3% of the time, Pallas kernels for 36%

profile of v1, /device:TPU:1, one launch (start us, length us, event | category | flops | bytes accessed | tf_op | source)
XLA Modules:
  0.0 126.9 jit_solution(3568009006779359354)
XLA Ops:
  0.0 7.7 %collective-permute-start.1 = (f32[16,512]{1,0:T(8,128)}, f32[16,512]{1,0:T(8,128)S(1)}, u32[]{:S(2)}, u32[]{:S(2)}) collective-permute-start(f32[16,512]{1,0:T(8,128)} %bitcast.246), channel_id=1, source_target_pairs={{0,4},{1,5},{2,6},{3,7},{4,0},{5,1},{6,2},{7,3},{8,12},{9,13},{10,... | collective-permute-start | bytes 98312 | tf_op jit(solution)/shard_map/ppermute | solution.py:265
  7.7 1.2 collective-permute-start
  8.9 2.4 %collective-permute-start.2 = (f32[16,512]{1,0:T(8,128)}, f32[16,512]{1,0:T(8,128)S(1)}, u32[]{:S(2)}, u32[]{:S(2)}) collective-permute-start(f32[16,512]{1,0:T(8,128)} %bitcast.248), channel_id=1, source_target_pairs={{0,6},{1,7},{2,0},{3,1},{4,2},{5,3},{6,4},{7,5},{8,14},{9,15},{10,... | collective-permute-start | bytes 98312 | tf_op jit(solution)/shard_map/ppermute | solution.py:265
  11.3 0.9 slice_bitcast_fusion.5
  12.2 0.9 slice_bitcast_fusion.3
  13.2 3.3 %collective-permute-start.7 = (bf16[3,2,4096]{2,1,0:T(2,128)(2,1)S(1)}, bf16[3,2,4096]{2,1,0:T(2,128)(2,1)S(1)}, u32[]{:S(2)}, u32[]{:S(2)}) collective-permute-start(bf16[3,2,4096]{2,1,0:T(2,128)(2,1)S(1)} %pad_maximum_fusion.3), channel_id=1, source_target_pairs={{0,1},{1,2},{2,3},{3,4},{4,5},{5,6},{6,7},{7,8},{8,9},{9,10},{10,1... | collective-permute-start | bytes 147464 | tf_op jit(solution)/shard_map/ppermute | solution.py:315
  17.2 6.5 %shard_map.145.sig_ref = f32[128,4096]{1,0:T(8,128)} custom-call(bf16[128,4096]{1,0:T(8,128)(2,1)} %k_ref.5, bf16[128,4096]{1,0:T(8,128)(2,1)} %v_ref.5, f32[3,3,4096]{2,1,0:T(4,128)} %f.7), custom_call_target="tpu_custom_call" | custom-call | flops 6291456 | bytes 4194304 | tf_op jit(solution)/shard_map/pallas_call | solution.py:54
  25.0 4.6 %shard_map.146 = (f32[4,16,512]{2,1,0:T(8,128)}, f32[128,4096]{1,0:T(8,128)}) custom-call(s32[2]{0:T(128)} %pad_add_fusion.place.p, f32[4,16,512]{2,1,0:T(8,128)} %copy-done.2, f32[128,4096]{1,0:T(8,128)} %shard_map.145.sig_ref, bf16[128,4096]{1,0:T(8,128)(2,1)} %k_ref.5, bf16[128,4096]{1,0:T(8,128)(2,1)} %v_ref.5, ...), custom_call_target="tpu_custom_call", output_to_operand_aliasing={{1}: (2, {})} | custom-call | flops 8388608 | bytes 1048576 | tf_op jit(solution)/shard_map/pallas_call | solution.py:93
  30.3 4.8 %shard_map.147 = (f32[4,16,512]{2,1,0:T(8,128)}, f32[128,4096]{1,0:T(8,128)}) custom-call(s32[2]{0:T(128)} %pad_add_fusion.place.p, f32[4,16,512]{2,1,0:T(8,128)} %copy-done, f32[128,4096]{1,0:T(8,128)} %get-tuple-element.17.sig_ref, bf16[128,4096]{1,0:T(8,128)(2,1)} %k_ref.5, bf16[128,4096]{1,0:T(8,128)(2,1)} %v_ref.5, ...), custom_call_target="tpu_custom_call", output_to_operand_aliasing={{1}: (2, {})} | custom-call | flops 8388608 | bytes 1048576 | tf_op jit(solution)/shard_map/pallas_call | solution.py:93
  35.1 1.1 select_add_fusion
  36.1 4.6 %collective-permute-start.9 = (f32[16,512]{1,0:T(8,128)S(1)}, f32[16,512]{1,0:T(8,128)S(1)}, u32[]{:S(2)}, u32[]{:S(2)}) collective-permute-start(f32[16,512]{1,0:T(8,128)S(1)} %get-tuple-element.33), channel_id=1, source_target_pairs={{0,6},{1,7},{2,0},{3,1},{4,2},{5,3},{6,4},{7,5},{8,14},{9,15},{10,... | collective-permute-start | bytes 98312 | tf_op jit(solution)/shard_map/ppermute | solution.py:265
  40.7 2.2 %collective-permute-start.10 = (f32[16,512]{1,0:T(8,128)S(1)}, f32[16,512]{1,0:T(8,128)S(1)}, u32[]{:S(2)}, u32[]{:S(2)}) collective-permute-start(f32[16,512]{1,0:T(8,128)S(1)} %get-tuple-element.35), channel_id=1, source_target_pairs={{0,4},{1,5},{2,6},{3,7},{4,0},{5,1},{6,2},{7,3},{8,12},{9,13},{10,... | collective-permute-start | bytes 98312 | tf_op jit(solution)/shard_map/ppermute | solution.py:265
  42.9 2.7 %collective-permute-done.11 = f32[16,512]{1,0:T(8,128)S(1)} collective-permute-done((f32[16,512]{1,0:T(8,128)S(1)}, f32[16,512]{1,0:T(8,128)S(1)}, u32[]{:S(2)}, u32[]{:S(2)}) %collective-permute-start.11) | collective-permute-done | bytes 32800 | tf_op jit(solution)/shard_map/ppermute | solution.py:265
  45.6 1.9 %collective-permute-done.10 = f32[16,512]{1,0:T(8,128)S(1)} collective-permute-done((f32[16,512]{1,0:T(8,128)S(1)}, f32[16,512]{1,0:T(8,128)S(1)}, u32[]{:S(2)}, u32[]{:S(2)}) %collective-permute-start.10) | collective-permute-done | bytes 32800 | tf_op jit(solution)/shard_map/ppermute | solution.py:265
  48.3 2.6 %collective-permute-start.14 = (f32[16,512]{1,0:T(8,128)S(1)}, f32[16,512]{1,0:T(8,128)S(1)}, u32[]{:S(2)}, u32[]{:S(2)}) collective-permute-start(f32[16,512]{1,0:T(8,128)S(1)} %fusion.36), channel_id=1, source_target_pairs={{0,24},{8,0},{16,8},{24,16},{32,56},{40,32},{48,40},{56,48},{64,88... | collective-permute-start | bytes 98312 | tf_op jit(solution)/shard_map/ppermute | solution.py:265
  51.9 3.3 %collective-permute-done.13 = f32[16,512]{1,0:T(8,128)S(1)} collective-permute-done((f32[16,512]{1,0:T(8,128)S(1)}, f32[16,512]{1,0:T(8,128)S(1)}, u32[]{:S(2)}, u32[]{:S(2)}) %collective-permute-start.13) | collective-permute-done | bytes 32800 | tf_op jit(solution)/shard_map/ppermute | solution.py:265
  56.3 2.7 %collective-permute-start.17 = (f32[16,512]{1,0:T(8,128)S(1)}, f32[16,512]{1,0:T(8,128)S(1)}, u32[]{:S(2)}, u32[]{:S(2)}) collective-permute-start(f32[16,512]{1,0:T(8,128)S(1)} %fusion.27), channel_id=1, source_target_pairs={{0,96},{8,104},{16,112},{24,120},{32,0},{40,8},{48,16},{56,24},{64... | collective-permute-start | bytes 98312 | tf_op jit(solution)/shard_map/ppermute | solution.py:265
  60.0 3.2 %collective-permute-done.16 = f32[16,512]{1,0:T(8,128)S(1)} collective-permute-done((f32[16,512]{1,0:T(8,128)S(1)}, f32[16,512]{1,0:T(8,128)S(1)}, u32[]{:S(2)}, u32[]{:S(2)}) %collective-permute-start.16) | collective-permute-done | bytes 32800 | tf_op jit(solution)/shard_map/ppermute | solution.py:265
  64.4 1.3 %collective-permute-start.18 = (f32[16,512]{1,0:T(8,128)S(1)}, f32[16,512]{1,0:T(8,128)S(1)}, u32[]{:S(2)}, u32[]{:S(2)}) collective-permute-start(f32[16,512]{1,0:T(8,128)S(1)} %fusion.17), channel_id=1, source_target_pairs={{0,128},{8,136},{16,144},{24,152},{32,160},{40,168},{48,176},{56,1... | collective-permute-start | bytes 98312 | tf_op jit(solution)/shard_map/ppermute | solution.py:265
  65.7 1.8 %collective-permute-start.4 = (f32[16,512]{1,0:T(8,128)S(1)}, f32[16,512]{1,0:T(8,128)S(1)}, u32[]{:S(2)}, u32[]{:S(2)}) collective-permute-start(f32[16,512]{1,0:T(8,128)S(1)} %get-tuple-element.37), channel_id=1, source_target_pairs={{0,4},{1,5},{2,6},{3,7},{4,0},{5,1},{6,2},{7,3},{8,12},{9,13},{10,... | collective-permute-start | bytes 98312 | tf_op jit(solution)/shard_map/ppermute | solution.py:265
  67.5 4.0 %collective-permute-start.3 = (f32[16,512]{1,0:T(8,128)S(1)}, f32[16,512]{1,0:T(8,128)S(1)}, u32[]{:S(2)}, u32[]{:S(2)}) collective-permute-start(f32[16,512]{1,0:T(8,128)S(1)} %get-tuple-element.37), channel_id=1, source_target_pairs={{0,2},{1,3},{2,4},{3,5},{4,6},{5,7},{6,0},{7,1},{8,10},{9,11},{10,... | collective-permute-start | bytes 98312 | tf_op jit(solution)/shard_map/ppermute | solution.py:265
  71.5 0.8 fusion.40
  72.9 2.1 %collective-permute-start.19 = (f32[16,512]{1,0:T(8,128)S(1)}, f32[16,512]{1,0:T(8,128)S(1)}, u32[]{:S(2)}, u32[]{:S(2)}) collective-permute-start(f32[16,512]{1,0:T(8,128)S(1)} %fusion.12), channel_id=1, source_target_pairs={{0,2},{1,3},{2,4},{3,5},{4,6},{5,7},{6,0},{7,1},{8,10},{9,11},{10,... | collective-permute-start | bytes 98312 | tf_op jit(solution)/shard_map/ppermute | solution.py:265
  75.1 3.4 %collective-permute-start.20 = (f32[16,512]{1,0:T(8,128)S(1)}, f32[16,512]{1,0:T(8,128)S(1)}, u32[]{:S(2)}, u32[]{:S(2)}) collective-permute-start(f32[16,512]{1,0:T(8,128)S(1)} %fusion.7), channel_id=1, source_target_pairs={{0,4},{1,5},{2,6},{3,7},{4,0},{5,1},{6,2},{7,3},{8,12},{9,13},{10,... | collective-permute-start | bytes 98312 | tf_op jit(solution)/shard_map/ppermute | solution.py:265
  78.5 6.9 %collective-permute-start.23 = (f32[4,16,512]{2,1,0:T(8,128)S(1)}, f32[4,16,512]{2,1,0:T(8,128)S(1)}, u32[]{:S(2)}, u32[]{:S(2)}) collective-permute-start(f32[4,16,512]{2,1,0:T(8,128)S(1)} %pad_maximum_fusion.1.w0.weight_ref), channel_id=1, source_target_pairs={{0,1},{1,0},{2,3},{3,2},{4,5},{5,4},{6,7},{7,6},{8,9},{9,8},{10,11... | collective-permute-start | bytes 393224 | tf_op jit(solution)/shard_map/ppermute | solution.py:265
  86.1 3.9 %collective-permute-start.22 = (f32[4,16,512]{2,1,0:T(8,128)S(1)}, f32[4,16,512]{2,1,0:T(8,128)S(1)}, u32[]{:S(2)}, u32[]{:S(2)}) collective-permute-start(f32[4,16,512]{2,1,0:T(8,128)S(1)} %get-tuple-element.32), channel_id=1, source_target_pairs={{0,1},{1,0},{2,3},{3,2},{4,5},{5,4},{6,7},{7,6},{8,9},{9,8},{10,11... | collective-permute-start | bytes 393224 | tf_op jit(solution)/shard_map/ppermute | solution.py:265
  90.7 6.3 %shard_map.148 = (f32[128,4096]{1,0:T(8,128)}, bf16[128,4096]{1,0:T(8,128)(2,1)}) custom-call(s32[2]{0:T(128)} %pad_add_fusion.place.p, f32[4,16,512]{2,1,0:T(8,128)} %copy-done.2, f32[4,16,512]{2,1,0:T(8,128)} %copy-done, f32[4,16,512]{2,1,0:T(8,128)} %copy-done.3, f32[4,16,512]{2,1,0:T(8,128)} %copy-done.4, f32[128,4096]{1,0:T(8,128)} %get-tuple-element.20.s.sig_ref, ...), custom_call_target="tpu_custom_call" | custom-call | flops 8388608 | bytes 2097152 | tf_op jit(solution)/shard_map/pallas_call | solution.py:182
  97.0 6.3 %shard_map.149 = (f32[128,4096]{1,0:T(8,128)}, bf16[128,4096]{1,0:T(8,128)(2,1)}) custom-call(s32[2]{0:T(128)} %pad_add_fusion.place.p, f32[4,16,512]{2,1,0:T(8,128)} %copy-done.2, f32[4,16,512]{2,1,0:T(8,128)} %copy-done, f32[4,16,512]{2,1,0:T(8,128)} %copy-done.3, f32[4,16,512]{2,1,0:T(8,128)} %copy-done.4, ...), custom_call_target="tpu_custom_call", output_to_operand_aliasing={{0}: (11, {}), {1}: (12, {})} | custom-call | flops 8388608 | bytes 2097152 | tf_op jit(solution)/shard_map/pallas_call | solution.py:182
  103.3 6.3 %shard_map.150 = (f32[128,4096]{1,0:T(8,128)}, bf16[128,4096]{1,0:T(8,128)(2,1)}) custom-call(s32[2]{0:T(128)} %pad_add_fusion.place.p, f32[4,16,512]{2,1,0:T(8,128)} %copy-done.2, f32[4,16,512]{2,1,0:T(8,128)} %copy-done, f32[4,16,512]{2,1,0:T(8,128)} %copy-done.3, f32[4,16,512]{2,1,0:T(8,128)} %copy-done.4, ...), custom_call_target="tpu_custom_call", output_to_operand_aliasing={{0}: (11, {}), {1}: (12, {})} | custom-call | flops 8388608 | bytes 2097152 | tf_op jit(solution)/shard_map/pallas_call | solution.py:182
  109.7 6.3 %shard_map.151 = (f32[128,4096]{1,0:T(8,128)}, bf16[128,4096]{1,0:T(8,128)(2,1)}) custom-call(s32[2]{0:T(128)} %pad_add_fusion.place.p, f32[4,16,512]{2,1,0:T(8,128)} %copy-done.2, f32[4,16,512]{2,1,0:T(8,128)} %copy-done, f32[4,16,512]{2,1,0:T(8,128)} %copy-done.3, f32[4,16,512]{2,1,0:T(8,128)} %copy-done.4, ...), custom_call_target="tpu_custom_call", output_to_operand_aliasing={{0}: (11, {}), {1}: (12, {})} | custom-call | flops 8388608 | bytes 2097152 | tf_op jit(solution)/shard_map/pallas_call | solution.py:182
  116.0 5.1 %shard_map.152.rest_0_ = bf16[128,4096]{1,0:T(8,128)(2,1)} custom-call(s32[2]{0:T(128)} %pad_add_fusion.place.p, f32[4,16,512]{2,1,0:T(8,128)} %copy-done, f32[4,16,512]{2,1,0:T(8,128)} %copy-done.4, f32[4,16,512]{2,1,0:T(8,128)} %get-tuple-element.31.state_ref, f32[128,4096]{1,0:T(8,128)} %get-tuple-element.27.conv_ref, ...), custom_call_target="tpu_custom_call" | custom-call | flops 8388608 | bytes 2097152 | tf_op jit(solution)/shard_map/pallas_call | solution.py:242
  121.8 5.1 %shard_map.153 = bf16[128,4096]{1,0:T(8,128)(2,1)} custom-call(s32[2]{0:T(128)} %pad_add_fusion.place.p, f32[4,16,512]{2,1,0:T(8,128)} %copy-done.2, f32[4,16,512]{2,1,0:T(8,128)} %copy-done.3, f32[4,16,512]{2,1,0:T(8,128)} %copy-done.7, f32[128,4096]{1,0:T(8,128)} %get-tuple-element.27.conv_ref, ...), custom_call_target="tpu_custom_call", output_to_operand_aliasing={{}: (8, {})} | custom-call | flops 8388608 | bytes 2097152 | tf_op jit(solution)/shard_map/pallas_call | solution.py:242
  (62 shorter events, 10.4 us)
Async XLA Ops:
  0.0 23.6 %collective-permute-start.1 = (f32[16,512]{1,0:T(8,128)}, f32[16,512]{1,0:T(8,128)S(1)}, u32[]{:S(2)}, u32[]{:S(2)}) collective-permute-start(f32[16,512]{1,0:T(8,128)} %bitcast.246), channel_id=1, source_target_pairs={{0,4},{1,5},{2,6},{3,7},{4,0},{5,1},{6,2},{7,3},{8,12},{9,13},{10,... | collective-permute-start | bytes 98312 | tf_op jit(solution)/shard_map/ppermute | solution.py:265
  7.7 15.9 %collective-permute-start = (f32[16,512]{1,0:T(8,128)}, f32[16,512]{1,0:T(8,128)S(1)}, u32[]{:S(2)}, u32[]{:S(2)}) collective-permute-start(f32[16,512]{1,0:T(8,128)} %bitcast.247), channel_id=1, source_target_pairs={{0,2},{1,3},{2,4},{3,5},{4,6},{5,7},{6,0},{7,1},{8,10},{9,11},{10,... | collective-permute-start | bytes 98312 | tf_op jit(solution)/shard_map/ppermute | solution.py:265
  8.9 14.7 %collective-permute-start.2 = (f32[16,512]{1,0:T(8,128)}, f32[16,512]{1,0:T(8,128)S(1)}, u32[]{:S(2)}, u32[]{:S(2)}) collective-permute-start(f32[16,512]{1,0:T(8,128)} %bitcast.248), channel_id=1, source_target_pairs={{0,6},{1,7},{2,0},{3,1},{4,2},{5,3},{6,4},{7,5},{8,14},{9,15},{10,... | collective-permute-start | bytes 98312 | tf_op jit(solution)/shard_map/ppermute | solution.py:265
  13.2 10.6 %collective-permute-start.7 = (bf16[3,2,4096]{2,1,0:T(2,128)(2,1)S(1)}, bf16[3,2,4096]{2,1,0:T(2,128)(2,1)S(1)}, u32[]{:S(2)}, u32[]{:S(2)}) collective-permute-start(bf16[3,2,4096]{2,1,0:T(2,128)(2,1)S(1)} %pad_maximum_fusion.3), channel_id=1, source_target_pairs={{0,1},{1,2},{2,3},{3,4},{4,5},{5,6},{6,7},{7,8},{8,9},{9,10},{10,1... | collective-permute-start | bytes 147464 | tf_op jit(solution)/shard_map/ppermute | solution.py:315
  17.2 6.5 %copy-start.8 = (f32[512,16]{0,1:T(8,128)S(1)}, f32[512,16]{0,1:T(8,128)}, u32[]{:S(2)}) copy-start(f32[512,16]{0,1:T(8,128)} %param.19) | copy-start | bytes 98308
  23.7 0.7 copy-start.2
  23.7 5.9 %collective-permute-start.6 = (f32[4,16,512]{2,1,0:T(8,128)S(1)}, f32[4,16,512]{2,1,0:T(8,128)S(1)}, u32[]{:S(2)}, u32[]{:S(2)}) collective-permute-start(f32[4,16,512]{2,1,0:T(8,128)S(1)} %pad_maximum_fusion.rate_ref.r0), channel_id=1, source_target_pairs={{0,1},{1,0},{2,3},{3,2},{4,5},{5,4},{6,7},{7,6},{8,9},{9,8},{10,11... | collective-permute-start | bytes 393224 | tf_op jit(solution)/shard_map/ppermute | solution.py:265
  29.6 5.5 %collective-permute-start.8 = (f32[4,16,512]{2,1,0:T(8,128)}, f32[4,16,512]{2,1,0:T(8,128)S(1)}, u32[]{:S(2)}, u32[]{:S(2)}) collective-permute-start(f32[4,16,512]{2,1,0:T(8,128)} %get-tuple-element.19), channel_id=1, source_target_pairs={{0,1},{1,0},{2,3},{3,2},{4,5},{5,4},{6,7},{7,6},{8,9},{9,8},{10,11... | collective-permute-start | bytes 393224 | tf_op jit(solution)/shard_map/ppermute | solution.py:265
  29.6 0.7 copy-start
  30.3 35.4 %copy-start.9 = (f32[512,16]{0,1:T(8,128)S(1)}, f32[512,16]{0,1:T(8,128)}, u32[]{:S(2)}) copy-start(f32[512,16]{0,1:T(8,128)} %param.20) | copy-start | bytes 98308
  35.0 37.4 %copy-start.1 = (f32[4,16,512]{2,1,0:T(8,128)S(1)}, f32[4,16,512]{2,1,0:T(8,128)}, u32[]{:S(2)}) copy-start(f32[4,16,512]{2,1,0:T(8,128)} %copy-done) | copy-start | bytes 393220
  35.0 50.4 %copy-start.6 = (f32[4,16,512]{2,1,0:T(8,128)S(1)}, f32[4,16,512]{2,1,0:T(8,128)}, u32[]{:S(2)}) copy-start(f32[4,16,512]{2,1,0:T(8,128)} %get-tuple-element.18) | copy-start | bytes 393220
  36.1 6.8 %collective-permute-start.9 = (f32[16,512]{1,0:T(8,128)S(1)}, f32[16,512]{1,0:T(8,128)S(1)}, u32[]{:S(2)}, u32[]{:S(2)}) collective-permute-start(f32[16,512]{1,0:T(8,128)S(1)} %get-tuple-element.33), channel_id=1, source_target_pairs={{0,6},{1,7},{2,0},{3,1},{4,2},{5,3},{6,4},{7,5},{8,14},{9,15},{10,... | collective-permute-start | bytes 98312 | tf_op jit(solution)/shard_map/ppermute | solution.py:265
  40.7 4.9 %collective-permute-start.11 = (f32[16,512]{1,0:T(8,128)S(1)}, f32[16,512]{1,0:T(8,128)S(1)}, u32[]{:S(2)}, u32[]{:S(2)}) collective-permute-start(f32[16,512]{1,0:T(8,128)S(1)} %get-tuple-element.34), channel_id=1, source_target_pairs={{0,2},{1,3},{2,4},{3,5},{4,6},{5,7},{6,0},{7,1},{8,10},{9,11},{10,... | collective-permute-start | bytes 98312 | tf_op jit(solution)/shard_map/ppermute | solution.py:265
  40.7 6.8 %collective-permute-start.10 = (f32[16,512]{1,0:T(8,128)S(1)}, f32[16,512]{1,0:T(8,128)S(1)}, u32[]{:S(2)}, u32[]{:S(2)}) collective-permute-start(f32[16,512]{1,0:T(8,128)S(1)} %get-tuple-element.35), channel_id=1, source_target_pairs={{0,4},{1,5},{2,6},{3,7},{4,0},{5,1},{6,2},{7,3},{8,12},{9,13},{10,... | collective-permute-start | bytes 98312 | tf_op jit(solution)/shard_map/ppermute | solution.py:265
  48.3 3.6 %collective-permute-start.14 = (f32[16,512]{1,0:T(8,128)S(1)}, f32[16,512]{1,0:T(8,128)S(1)}, u32[]{:S(2)}, u32[]{:S(2)}) collective-permute-start(f32[16,512]{1,0:T(8,128)S(1)} %fusion.36), channel_id=1, source_target_pairs={{0,24},{8,0},{16,8},{24,16},{32,56},{40,32},{48,40},{56,48},{64,88... | collective-permute-start | bytes 98312 | tf_op jit(solution)/shard_map/ppermute | solution.py:265
  50.8 4.3 %collective-permute-start.13 = (f32[16,512]{1,0:T(8,128)S(1)}, f32[16,512]{1,0:T(8,128)S(1)}, u32[]{:S(2)}, u32[]{:S(2)}) collective-permute-start(f32[16,512]{1,0:T(8,128)S(1)} %fusion.36), channel_id=1, source_target_pairs={{0,16},{8,24},{16,0},{24,8},{32,48},{40,56},{48,32},{56,40},{64,80... | collective-permute-start | bytes 98312 | tf_op jit(solution)/shard_map/ppermute | solution.py:265
  51.4 4.1 %collective-permute-start.12 = (f32[16,512]{1,0:T(8,128)S(1)}, f32[16,512]{1,0:T(8,128)S(1)}, u32[]{:S(2)}, u32[]{:S(2)}) collective-permute-start(f32[16,512]{1,0:T(8,128)S(1)} %fusion.36), channel_id=1, source_target_pairs={{0,8},{8,16},{16,24},{24,0},{32,40},{40,48},{48,56},{56,32},{64,72... | collective-permute-start | bytes 98312 | tf_op jit(solution)/shard_map/ppermute | solution.py:265
  56.3 3.7 %collective-permute-start.17 = (f32[16,512]{1,0:T(8,128)S(1)}, f32[16,512]{1,0:T(8,128)S(1)}, u32[]{:S(2)}, u32[]{:S(2)}) collective-permute-start(f32[16,512]{1,0:T(8,128)S(1)} %fusion.27), channel_id=1, source_target_pairs={{0,96},{8,104},{16,112},{24,120},{32,0},{40,8},{48,16},{56,24},{64... | collective-permute-start | bytes 98312 | tf_op jit(solution)/shard_map/ppermute | solution.py:265
  58.9 4.3 %collective-permute-start.16 = (f32[16,512]{1,0:T(8,128)S(1)}, f32[16,512]{1,0:T(8,128)S(1)}, u32[]{:S(2)}, u32[]{:S(2)}) collective-permute-start(f32[16,512]{1,0:T(8,128)S(1)} %fusion.27), channel_id=1, source_target_pairs={{0,64},{8,72},{16,80},{24,88},{32,96},{40,104},{48,112},{56,120},{... | collective-permute-start | bytes 98312 | tf_op jit(solution)/shard_map/ppermute | solution.py:265
  59.4 4.1 %collective-permute-start.15 = (f32[16,512]{1,0:T(8,128)S(1)}, f32[16,512]{1,0:T(8,128)S(1)}, u32[]{:S(2)}, u32[]{:S(2)}) collective-permute-start(f32[16,512]{1,0:T(8,128)S(1)} %fusion.27), channel_id=1, source_target_pairs={{0,32},{8,40},{16,48},{24,56},{32,64},{40,72},{48,80},{56,88},{64,... | collective-permute-start | bytes 98312 | tf_op jit(solution)/shard_map/ppermute | solution.py:265
  64.4 7.2 %collective-permute-start.18 = (f32[16,512]{1,0:T(8,128)S(1)}, f32[16,512]{1,0:T(8,128)S(1)}, u32[]{:S(2)}, u32[]{:S(2)}) collective-permute-start(f32[16,512]{1,0:T(8,128)S(1)} %fusion.17), channel_id=1, source_target_pairs={{0,128},{8,136},{16,144},{24,152},{32,160},{40,168},{48,176},{56,1... | collective-permute-start | bytes 98312 | tf_op jit(solution)/shard_map/ppermute | solution.py:265
  65.7 9.3 %collective-permute-start.4 = (f32[16,512]{1,0:T(8,128)S(1)}, f32[16,512]{1,0:T(8,128)S(1)}, u32[]{:S(2)}, u32[]{:S(2)}) collective-permute-start(f32[16,512]{1,0:T(8,128)S(1)} %get-tuple-element.37), channel_id=1, source_target_pairs={{0,4},{1,5},{2,6},{3,7},{4,0},{5,1},{6,2},{7,3},{8,12},{9,13},{10,... | collective-permute-start | bytes 98312 | tf_op jit(solution)/shard_map/ppermute | solution.py:265
  67.5 11.0 %collective-permute-start.3 = (f32[16,512]{1,0:T(8,128)S(1)}, f32[16,512]{1,0:T(8,128)S(1)}, u32[]{:S(2)}, u32[]{:S(2)}) collective-permute-start(f32[16,512]{1,0:T(8,128)S(1)} %get-tuple-element.37), channel_id=1, source_target_pairs={{0,2},{1,3},{2,4},{3,5},{4,6},{5,7},{6,0},{7,1},{8,10},{9,11},{10,... | collective-permute-start | bytes 98312 | tf_op jit(solution)/shard_map/ppermute | solution.py:265
  71.5 7.0 %collective-permute-start.5 = (f32[16,512]{1,0:T(8,128)S(1)}, f32[16,512]{1,0:T(8,128)S(1)}, u32[]{:S(2)}, u32[]{:S(2)}) collective-permute-start(f32[16,512]{1,0:T(8,128)S(1)} %get-tuple-element.37), channel_id=1, source_target_pairs={{0,6},{1,7},{2,0},{3,1},{4,2},{5,3},{6,4},{7,5},{8,14},{9,15},{10,... | collective-permute-start | bytes 98312 | tf_op jit(solution)/shard_map/ppermute | solution.py:265
  72.4 13.0 %collective-permute-start.21 = (f32[16,512]{1,0:T(8,128)S(1)}, f32[16,512]{1,0:T(8,128)S(1)}, u32[]{:S(2)}, u32[]{:S(2)}) collective-permute-start(f32[16,512]{1,0:T(8,128)S(1)} %fusion.2), channel_id=1, source_target_pairs={{0,6},{1,7},{2,0},{3,1},{4,2},{5,3},{6,4},{7,5},{8,14},{9,15},{10,... | collective-permute-start | bytes 98312 | tf_op jit(solution)/shard_map/ppermute | solution.py:265
  72.9 12.5 %collective-permute-start.19 = (f32[16,512]{1,0:T(8,128)S(1)}, f32[16,512]{1,0:T(8,128)S(1)}, u32[]{:S(2)}, u32[]{:S(2)}) collective-permute-start(f32[16,512]{1,0:T(8,128)S(1)} %fusion.12), channel_id=1, source_target_pairs={{0,2},{1,3},{2,4},{3,5},{4,6},{5,7},{6,0},{7,1},{8,10},{9,11},{10,... | collective-permute-start | bytes 98312 | tf_op jit(solution)/shard_map/ppermute | solution.py:265
  75.1 10.4 %collective-permute-start.20 = (f32[16,512]{1,0:T(8,128)S(1)}, f32[16,512]{1,0:T(8,128)S(1)}, u32[]{:S(2)}, u32[]{:S(2)}) collective-permute-start(f32[16,512]{1,0:T(8,128)S(1)} %fusion.7), channel_id=1, source_target_pairs={{0,4},{1,5},{2,6},{3,7},{4,0},{5,1},{6,2},{7,3},{8,12},{9,13},{10,... | collective-permute-start | bytes 98312 | tf_op jit(solution)/shard_map/ppermute | solution.py:265
  78.5 11.5 %copy-start.3 = (f32[4,16,512]{2,1,0:T(8,128)}, f32[4,16,512]{2,1,0:T(8,128)S(1)}, u32[]{:S(2)}) copy-start(f32[4,16,512]{2,1,0:T(8,128)S(1)} %pad_maximum_fusion.1.w0.weight_ref) | copy-start | bytes 393220
  78.5 11.5 %collective-permute-start.23 = (f32[4,16,512]{2,1,0:T(8,128)S(1)}, f32[4,16,512]{2,1,0:T(8,128)S(1)}, u32[]{:S(2)}, u32[]{:S(2)}) collective-permute-start(f32[4,16,512]{2,1,0:T(8,128)S(1)} %pad_maximum_fusion.1.w0.weight_ref), channel_id=1, source_target_pairs={{0,1},{1,0},{2,3},{3,2},{4,5},{5,4},{6,7},{7,6},{8,9},{9,8},{10,11... | collective-permute-start | bytes 393224 | tf_op jit(solution)/shard_map/ppermute | solution.py:265
  86.1 35.0 %collective-permute-start.22 = (f32[4,16,512]{2,1,0:T(8,128)S(1)}, f32[4,16,512]{2,1,0:T(8,128)S(1)}, u32[]{:S(2)}, u32[]{:S(2)}) collective-permute-start(f32[4,16,512]{2,1,0:T(8,128)S(1)} %get-tuple-element.32), channel_id=1, source_target_pairs={{0,1},{1,0},{2,3},{3,2},{4,5},{5,4},{6,7},{7,6},{8,9},{9,8},{10,11... | collective-permute-start | bytes 393224 | tf_op jit(solution)/shard_map/ppermute | solution.py:265
  121.1 0.7 copy-start.7
  (2 other events, 1.3 us)

commit v2 on v0

v2 whole, which is shorter than its diff:
```python
import functools

import jax
import jax.numpy as jnp
import numpy as np
from jax import lax
from jax.experimental import pallas as pl
from jax.experimental.pallas import tpu as pltpu
from jax.sharding import PartitionSpec as P

F32, BF16 = jnp.float32, jnp.bfloat16
NH = 4
LANE = 128
VMEM = pl.BlockSpec(memory_space=pltpu.VMEM)
ANY = pl.BlockSpec(memory_space=pl.ANY)
HBM = pl.BlockSpec(memory_space=pltpu.HBM)
GRANT = pltpu.CompilerParams(vmem_limit_bytes=60 << 20)


def two_parts(value):
    high = value.astype(BF16)
    return high, (value - high.astype(F32)).astype(BF16)


def transforms(rows):
    k = np.arange(rows)[:, None]
    n = np.arange(rows)[None, :]
    angle = np.pi * (((2 * k + 1) * n) % (4 * rows)) / (2 * rows)
    forward = np.concatenate([np.cos(angle), -np.sin(angle)], axis=0).astype(np.float32)
    inverse = (np.concatenate([np.cos(angle).T, -np.sin(angle).T], axis=1) / rows).astype(np.float32)
    bf16 = jnp.bfloat16

    def parts(array):
        high = array.astype(bf16)
        return high, (array - high.astype(np.float32)).astype(bf16)

    fh, fl = parts(forward)
    gh, gl = parts(inverse)
    return np.concatenate([fh, fl, fh], axis=1), np.concatenate([gh, gl, gh], axis=1)


def rounded(value):
    return value.astype(BF16).astype(F32)


def mix(now, one, two, taps):
    return taps[0:1] * now + taps[1:2] * one + taps[2:3] * two


def mix_top(block, edge, taps):
    a, b = block[0:1], block[1:2]
    e0, e1 = edge[0:1], edge[1:2]
    return mix(a, e1, e0, taps), mix(b, a, e1, taps)


def top_rows(first, second, rest):
    row = lax.broadcasted_iota(jnp.int32, rest.shape, 0)
    return jnp.where(row == 0, first, jnp.where(row == 1, second, rest))


def shifts(rows):
    return np.concatenate([np.roll(np.eye(rows), n, axis=0) for n in range(3)], axis=0).astype(jnp.bfloat16)


def mix_shifted(shift, block, taps):
    rows = block.shape[0]
    parts = jnp.dot(shift, block, preferred_element_type=F32)
    return mix(parts[:rows], parts[rows : 2 * rows], parts[2 * rows :], taps)


def edge_kernel(q_ref, k_ref, v_ref, edge_ref, last, sems):
    mover = Mover(sems)
    rows = q_ref.shape[0]
    copies = [
        mover.start(ref.at[rows - 16 : rows], last.at[n]) for n, ref in enumerate((q_ref, k_ref, v_ref))
    ]
    for copy in copies:
        copy.wait()
    for at in range(0, edge_ref.shape[1], 512):
        lanes = slice(at, at + 512)
        two = [last[n, :, lanes].astype(F32)[14:] for n in range(3)]
        edge_ref[:, lanes] = jnp.concatenate(two + [two[0]], axis=0)


def edge_call(q_proj, k_proj, v_proj):
    width = q_proj.shape[1]
    return pl.pallas_call(
        edge_kernel,
        in_specs=[ANY, ANY, ANY],
        out_specs=VMEM,
        out_shape=jax.ShapeDtypeStruct((8, width), F32),
        scratch_shapes=[pltpu.VMEM((3, 16, width), BF16), pltpu.SemaphoreType.DMA((3,))],
        compiler_params=GRANT,
        cost_estimate=cost(1 << 20),
    )(q_proj, k_proj, v_proj)


def signal_kernel(k_any, v_any, filt_any, sig_any, k, v, filt, line, sig, sems):
    mover = Mover(sems)
    rows, width = k.shape
    group = 512
    parts = [slice(at, at + group) for at in range(0, width, group)]
    small = [mover.start(filt_any.at[1:3], filt)]
    fetched = [
        (mover.start(k_any.at[:, at], k.at[:, at]), mover.start(v_any.at[:, at], v.at[:, at])) for at in parts
    ]
    for copy in small:
        copy.wait()
    line[:, 0:8, :] = jnp.zeros((4, 8, LANE), F32)

    def short(array, taps, slot, here):
        line[slot, 8:, :] = array[:, here].astype(F32)
        return mix(line[slot, 8:, :], line[slot, 7 : rows + 7, :], line[slot, 6 : rows + 6, :], taps)

    sent = []
    for at, copies in zip(parts, fetched):
        for copy in copies:
            copy.wait()
        for lane in range(at.start, at.stop, LANE):
            here = slice(lane, lane + LANE)
            slot = lane // LANE % 2 * 2
            key = short(k, filt[0, :, here], slot, here)
            value = short(v, filt[1, :, here], slot + 1, here)
            sig[:, here] = (key * value).astype(BF16)
        sent.append(mover.start(sig.at[:, at], sig_any.at[:, at]))
    for copy in sent:
        copy.wait()


def signal_call(k_proj, v_proj, filt):
    rows, width = k_proj.shape
    whole = ((rows, width), BF16)
    return run(
        signal_kernel,
        k_proj, v_proj, filt,
        out=[whole],
        scratch=[whole, whole, ((2, 3, width), F32), ((4, rows + 8, LANE), F32), whole],
        copies=1 + 3 * (width // 512),
        flops=rows * width * 12,
    )[0]


def where_am_i():
    ch = lax.axis_index("ch")
    return ch // 2, lax.rem(ch, 2), lax.axis_index("seq") * 2 * NH + ch


def cost(flops):
    return pl.CostEstimate(flops=flops, bytes_accessed=1 << 20, transcendentals=0)


def run(kernel, *operands, out, scratch=(), copies=1, flops=1 << 20, near=(), near_out=()):
    operands = [
        pltpu.with_memory_space_constraint(value, pltpu.VMEM if n in near else pltpu.HBM)
        for n, value in enumerate(operands)
    ]
    return pl.pallas_call(
        kernel,
        in_specs=[VMEM if n in near else HBM for n in range(len(operands))],
        out_specs=[VMEM if n in near_out else HBM for n in range(len(out))],
        out_shape=[
            pltpu.VMEM(*shape) if n in near_out else pltpu.HBM(*shape)
            for n, shape in enumerate(out)
        ],
        scratch_shapes=[*[pltpu.VMEM(*shape) for shape in scratch], pltpu.SemaphoreType.DMA((copies,))],
        compiler_params=pltpu.CompilerParams(vmem_limit_bytes=(24 if near or near_out else 60) << 20),
        cost_estimate=cost(flops),
    )(*operands)


class Mover:
    def __init__(self, sems):
        self.sems, self.used = sems, 0

    def start(self, source, target):
        copy = pltpu.make_async_copy(source, target, self.sems.at[self.used])
        self.used += 1
        copy.start()
        return copy


def param_at(place, chip):
    return lax.rem(place[0] + NH - chip, NH)


def params_of(place, chip, parity, par0, par1, rows):
    which = param_at(place, chip)
    return jnp.where(place[1] == parity, par0[which, rows, :], par1[which, rows, :])


def weights_of(rates, residues):
    gap = -2.0 * rates
    series = 1.0 + gap * (0.5 + gap * (1 / 6 + gap * (1 / 24 + gap * (1 / 120 + gap * (1 / 720)))))
    return residues * jnp.sqrt(-jnp.where(gap > -0.1, gap * series, jnp.exp(gap) - 1.0))


def fetch_params(mover, arrays, par0, par1):
    return [
        mover.start(array, (par0, par1)[n // NH].at[n % NH]) for n, array in enumerate(arrays)
    ]


def states(rates, first, second, sig_ref, at):
    rows = sig_ref.shape[0]
    half = rows // 2
    decay = jnp.exp(-rates)
    early = first * decay + second
    late = sig_ref[half : half + 1, at] * decay + sig_ref[half + 1 : half + 2, at]
    for t in range(2, half):
        early = early * decay + sig_ref[t : t + 1, at]
        late = late * decay + sig_ref[half + t : half + t + 1, at]
    return early * jnp.exp(-rates * half) + late


def own_decay(place, par0, par1, span):
    modes, group = par0.shape[1] // 2, par0.shape[2]
    per_group = modes * group // (2 * LANE)
    mine = place[2]
    chip, parity = mine // (2 * per_group), lax.rem(mine // per_group, 2)
    mode, part = lax.rem(mine, per_group) // 2, lax.rem(mine, 2)
    at = pl.ds(pl.multiple_of(part * (group // 2), group // 2), group // 2)
    which = param_at(place, chip)
    rate = jnp.where(
        parity == place[1], par0[which, pl.ds(mode, 1), at], par1[which, pl.ds(mode, 1), at]
    )
    row = lax.broadcasted_iota(jnp.int32, (8, LANE), 0)
    return jnp.exp(-span * jnp.where(lax.rem(row, 2) == 0, rate[:, :LANE], rate[:, LANE:]))


def state_kernel(*refs):
    pars, (sig_any, k_any, v_any, edge, filt_any, state, top_any, decay) = refs[: 2 * NH], refs[2 * NH : 2 * NH + 8]
    par0, par1, packed, k_top, v_top, filt, sig, top, sems = refs[2 * NH + 8 :]
    place = where_am_i()
    mover = Mover(sems)
    modes, group = par0.shape[1] // 2, par0.shape[2]
    width = top.shape[1]
    blocks = group // LANE
    small = [
        mover.start(filt_any.at[1:3], filt),
        mover.start(k_any.at[0:16], k_top),
        mover.start(v_any.at[0:16], v_top),
    ]
    for n, array in enumerate(pars):
        (par0, par1)[n // NH][n % NH] = array[...]
    parts = [slice(at, at + group) for at in range(0, width, group)]
    signals = [mover.start(sig_any.at[:, at], packed.at[:, at]) for at in parts]
    for copy in small:
        copy.wait()
    for n, at in enumerate(parts):
        signals[n].wait()
        sig[...] = packed[:, at].astype(F32)
        key = mix_top(k_top[:, at].astype(F32), edge[2:4, at], filt[0, :, at])
        value = mix_top(v_top[:, at].astype(F32), edge[4:6, at], filt[1, :, at])
        s0, s1 = rounded(key[0] * value[0]), rounded(key[1] * value[1])
        top[:, at] = top_rows(s0, s1, sig[0:16, :]).astype(BF16)
        rates = params_of(place, n // 2, n % 2, par0, par1, slice(0, modes))
        value = states(rates, s0, s1, sig, slice(0, group))
        base = n * modes * blocks
        for j in range(blocks):
            state[pl.ds(base + j, modes, stride=blocks), :] = value[:, j * LANE : (j + 1) * LANE]
    sent = mover.start(top, top_any)
    decay[...] = own_decay(place, par0, par1, float(sig.shape[0]))
    sent.wait()


def state_call(pars, sig, k_proj, v_proj, edges, filt):
    rows, width = k_proj.shape
    modes, group = pars[0].shape[0] // 2, pars[0].shape[1]
    par = ((NH, 2 * modes, group), F32)
    count = modes * width // LANE
    return run(
        state_kernel,
        *pars, sig, k_proj, v_proj, edges, filt,
        out=[((count, LANE), F32), ((16, width), BF16), ((8, LANE), F32)],
        scratch=[
            par, par, ((rows, width), BF16), ((16, width), BF16), ((16, width), BF16),
            ((2, 3, width), F32), ((rows, group), F32), ((16, width), BF16),
        ],
        near=[*range(2 * NH), 2 * NH + 3],
        near_out=[0, 2],
        copies=4 + width // group,
        flops=rows * width * modes * 2,
    )


def scan_kernel(got_ref, decay_ref, out_ref, _):
    decay = decay_ref[0:2, :]
    total = jnp.zeros((2, LANE), F32)
    for n in range(got_ref.shape[0]):
        out_ref[n] = total
        total = total * decay + got_ref[n]


def scan_call(got, decay):
    return run(scan_kernel, got, decay, out=[(got.shape, F32)], near=[0, 1], near_out=[0], flops=got.size * 2)[0]


def decaying_sum(start_ref, rate_ref, step_ref, at, first, store, rows):
    modes = start_ref.shape[0]
    ramp = lax.broadcasted_iota(jnp.int32, (8, LANE), 0).astype(F32) + first
    terms = [start_ref[m : m + 1, at] * jnp.exp(-rate_ref[m : m + 1, at] * ramp) for m in range(modes)]
    steps = [jnp.broadcast_to(step_ref[m : m + 1, at], (8, LANE)) for m in range(modes)]
    for tile in range(rows // 8):
        total = terms
        while len(total) > 1:
            total = [a + b for a, b in zip(total[::2], total[1::2])]
        store(slice(tile * 8, tile * 8 + 8), total[0])
        if tile + 1 < rows // 8:
            terms = [a * b for a, b in zip(terms, steps)]


def local_kernel(first, *refs):
    sig_ref, top_ref, q_ref, edge_ref, filt_ref, fwd_ref, inv_ref, shift_ref, conv_ref, query_ref = refs[2 * NH : 2 * NH + 10]
    par0, par1, taps_ref, rate_s, step_s, weight_s, sems = refs[2 * NH + 10 :]
    place = where_am_i()
    rows, group = sig_ref.shape
    modes = par0.shape[1] // 2
    step = pl.program_id(0) + first
    chip, parity = step // 2, lax.rem(step, 2)

    @pl.when(pl.program_id(0) == 0)
    def _():
        for copy in fetch_params(Mover(sems), refs[: 2 * NH], par0, par1):
            copy.wait()

    rate_s[...] = params_of(place, chip, parity, par0, par1, slice(0, modes))
    weight_s[...] = weights_of(
        rate_s[...], params_of(place, chip, parity, par0, par1, slice(modes, 2 * modes))
    )
    step_s[...] = jnp.exp(-8.0 * rate_s[...])

    def body(n, _):
        lanes = pl.ds(pl.multiple_of(n * LANE, LANE), LANE)

        def store(tile, value):
            taps_ref[tile, lanes] = value

        decaying_sum(weight_s, rate_s, step_s, lanes, 0.0, store, rows)
        return 0

    lax.fori_loop(0, group // LANE, body, 0)
    x = jnp.concatenate([top_ref[...], sig_ref[16:, :]], axis=0)
    th, tl = two_parts(taps_ref[...])
    sig = jnp.dot(fwd_ref[:, : 2 * rows], jnp.concatenate([x, x], axis=0), preferred_element_type=F32)
    fil = jnp.dot(fwd_ref[...], jnp.concatenate([th, th, tl], axis=0), preferred_element_type=F32)
    sr, si, fr, fi = sig[:rows], sig[rows:], fil[:rows], fil[rows:]
    ph, pw = two_parts(jnp.concatenate([sr * fr - si * fi, sr * fi + si * fr], axis=0))
    conv_ref[...] = jnp.dot(
        inv_ref[...], jnp.concatenate([ph, ph, pw], axis=0), preferred_element_type=F32
    )
    query = mix_shifted(shift_ref[...], q_ref[...], filt_ref[0])
    q0, q1 = mix_top(q_ref[0:16, :].astype(F32), edge_ref[0:2, :], filt_ref[0])
    query_ref[...] = top_rows(q0, q1, query).astype(BF16)


def local_call(half, pars, sig, top, q_proj, edges, filt, fwd, inv, shift):
    rows, width = q_proj.shape
    modes, group = pars[0].shape[0] // 2, pars[0].shape[1]
    par = pltpu.VMEM((NH, 2 * modes, group), F32)
    first = half * NH

    def lanes(n):
        return (0, n + first)

    def whole(array):
        return pl.BlockSpec(array.shape, lambda n: (0,) * array.ndim)

    block = pl.BlockSpec((rows, group), lambda n: (0, n))
    return pl.pallas_call(
        functools.partial(local_kernel, first),
        grid=(NH,),
        in_specs=[ANY] * (2 * NH) + [
            pl.BlockSpec((rows, group), lanes), pl.BlockSpec((16, group), lanes), pl.BlockSpec((rows, group), lanes),
            pl.BlockSpec((8, group), lanes), pl.BlockSpec((3, 3, group), lambda n: (0, 0, n + first)),
            whole(fwd), whole(inv), whole(shift),
        ],
        out_specs=[block, block],
        out_shape=[
            jax.ShapeDtypeStruct((rows, width // 2), F32),
            jax.ShapeDtypeStruct((rows, width // 2), BF16),
        ],
        scratch_shapes=[par, par, pltpu.VMEM((rows, group), F32)]
        + [pltpu.VMEM((modes, group), F32)] * 3 + [pltpu.SemaphoreType.DMA((2 * NH,))],
        compiler_params=GRANT,
        cost_estimate=cost(rows * rows * group * 16 * NH),
    )(*pars, sig, top, q_proj, edges, filt, fwd, inv, shift)


def carry_kernel(*refs):
    pars, (state, top_any, skip_any, sig_any) = refs[: 2 * NH], refs[2 * NH : 2 * NH + 4]
    conv_anys, query_anys = refs[2 * NH + 4 : 2 * NH + 6], refs[2 * NH + 6 : 2 * NH + 8]
    out_any, par0, par1, sig, top, skip, conv, query, out, start_s, step_s, rate_s, sems = refs[2 * NH + 8 :]
    place = where_am_i()
    mover = Mover(sems)
    rows, width = sig.shape
    modes, group = par0.shape[1] // 2, par0.shape[2]
    blocks = group // LANE
    small = [
        *fetch_params(mover, pars, par0, par1),
        mover.start(top_any, top),
        mover.start(skip_any, skip),
    ]
    span = width // 2
    parts = [slice(at, at + group) for at in range(0, width, group)]
    fetched = []
    for at in parts:
        n, inside = at.start // span, slice(at.start % span, at.start % span + group)
        fetched.append(
            [
                mover.start(conv_anys[n].at[:, inside], conv.at[:, at]),
                mover.start(query_anys[n].at[:, inside], query.at[:, at]),
                mover.start(sig_any.at[:, at], sig.at[:, at]),
            ]
        )
    for copy in small:
        copy.wait()
    sent = []
    for n, at in enumerate(parts):
        rate_s[...] = params_of(place, n // 2, n % 2, par0, par1, slice(0, modes))
        step_s[...] = jnp.exp(-8.0 * rate_s[...])
        weights = weights_of(
            rate_s[...], params_of(place, n // 2, n % 2, par0, par1, slice(modes, 2 * modes))
        )
        for j in range(blocks):
            lanes = slice(j * LANE, (j + 1) * LANE)
            from_state = state[pl.ds(n * modes * blocks + j, modes, stride=blocks), :]
            start_s[:, lanes] = weights[:, lanes] * from_state
        for copy in fetched[n]:
            copy.wait()

        def body(j, _):
            lanes = pl.ds(pl.multiple_of(j * LANE, LANE), LANE)
            here = pl.ds(pl.multiple_of(at.start + j * LANE, LANE), LANE)
            direct = skip[:, here]
            held = []

            def store(tile, value):
                held.append(rounded(conv[tile, here] + value))
                if len(held) == 2:
                    both = slice(tile.start - 8, tile.stop)
                    signal = (top[:, here] if both.start == 0 else sig[both, here]).astype(F32)
                    total = jnp.concatenate(held, axis=0) + direct * signal
                    out[both, here] = (query[both, here].astype(F32) * total).astype(BF16)
                    held.clear()

            decaying_sum(start_s, rate_s, step_s, lanes, 1.0, store, rows)
            return 0

        lax.fori_loop(0, blocks, body, 0)
        sent.append(mover.start(out.at[:, at], out_any.at[:, at]))
    for copy in sent:
        copy.wait()


def carry_call(pars, states, top, skip, sig, convs, queries):
    rows, width = sig.shape
    modes, group = pars[0].shape[0] // 2, pars[0].shape[1]
    par, half = ((NH, 2 * modes, group), F32), ((rows, width), BF16)
    return run(
        carry_kernel,
        *pars, states, top, skip, sig, *convs, *queries,
        out=[half],
        scratch=[
            par, par, half, (top.shape, BF16), (skip.shape, F32),
            ((rows, width), F32), half, half,
        ] + [((modes, group), F32)] * 3,
        near=[2 * NH],
        copies=2 + 2 * NH + 4 * (width // group),
        flops=rows * width * modes * 2,
    )[0]


def moved(value, target):
    return lax.ppermute(value, "ch", [(i, target(i)) for i in range(2 * NH)])


def to_chip(value, by):
    return moved(value, lambda i: (i + 2 * by) % (2 * NH))


def to_core(value):
    return moved(value, lambda i: i ^ 1)


def after(value, *others):
    return lax.optimization_barrier((value, *others))[0]


def on_device(q_proj, k_proj, v_proj, short_filter, rates, residues, skip):
    rows, width = q_proj.shape
    everyone = ("seq", "ch")
    total = lax.axis_size(everyone)
    fwd, inv = (jnp.asarray(a) for a in transforms(rows))
    shift = jnp.asarray(shifts(rows))

    own = jnp.concatenate([rates.T, residues.T], axis=0)
    far = to_chip(own, 2)
    edges = edge_call(q_proj, k_proj, v_proj)
    one = to_chip(after(own, edges), 1)
    edges = lax.ppermute(edges, everyone, [(i, i + 1) for i in range(total - 1)])
    three = to_chip(own, 3)
    sig = signal_call(k_proj, v_proj, short_filter)
    mine = [own, one, far, three]
    pars = mine + [to_core(own)] + [to_core(after(value, sig)) for value in mine[1:]]
    states, top, decay = state_call(pars, sig, k_proj, v_proj, edges, short_filter)

    def exchange(value):
        return lax.all_to_all(value, everyone, 0, 0, tiled=True)

    def local(half):
        return local_call(half, pars, sig, top, q_proj, edges, short_filter, fwd, inv, shift)

    got = exchange(states.reshape(total, -1, LANE))
    got, *early = lax.optimization_barrier((got, *local(0)))
    carry = exchange(scan_call(got, decay))
    carry, *late = lax.optimization_barrier((carry, *local(1)))
    convs, queries = zip(early, late)
    return carry_call(pars, carry.reshape(states.shape), top, skip[None, :], sig, convs, queries)


def solution(mesh):
    placed = (
        P(("seq", "ch"), None),
        P(("seq", "ch"), None),
        P(("seq", "ch"), None),
        P(),
        P("ch", None),
        P("ch", None),
        P(),
    )
    return jax.shard_map(
        on_device, mesh=mesh, in_specs=placed, out_specs=P(("seq", "ch"), None), check_vma=False
    )
```

time: 650 us -> 83.5 us (0.13); the launches traced: 640 us -> 83 us
  matrix products: 190 us -> 0 us
  waiting for transfers between devices: 199 us -> 16.5 us
  local copies, waits for them, and re-layouts: 88 us -> 0.04 us
  starting transfers between devices: 96 us -> 32.5 us
  other arithmetic: 43.2 us -> 0.78 us
  Pallas kernels: 0 us -> 32.8 us
  blocking collectives: 21.9 us -> 0 us
    dot_general x30 -> x0, matrix products: 190 us -> none  [the longest x2 18.6 us: columns_forward(): jnp.einsum('jp,kpqc->kjqc', sin_p, real, precision=HIGHEST)]
    all_to_all x10 -> x2, waiting for transfers between devices: 199 us -> 15.6 us  [exchange(): return lax.all_to_all(value, everyone, 0, 0, tiled=True)]
    all_to_all x10 -> x2, starting transfers between devices: 89.7 us -> 15.3 us  [exchange(): return lax.all_to_all(value, everyone, 0, 0, tiled=True)]
    pallas_call x0 -> x7, Pallas kernels: none -> 32.8 us  [the longest x2 15.7 us: local_call(): pl.pallas_call(functools.partial(local_kernel, first), grid=(NH,), in_spe...]
    all_to_all x8 -> x0, local copies, waits for them, and re-layouts: 30.7 us -> none  [the longest x3 14.3 us: on_device(): lax.all_to_all(back_re, 'seq', split_axis=1, concat_axis=0, tiled=True)]
    all_to_all x1 -> x0, blocking collectives: 21.9 us -> none  [on_device(): lax.all_to_all(conv_rows, 'seq', split_axis=0, concat_axis=1, tiled=True)[0]]
    add x19 -> x0, other arithmetic: 18.9 us -> none  [the longest x16 15.8 us: add_mode(): return total + scale[None, :] * jnp.exp(-rate[None, :] * times[:, None])]
    convert_element_type x6 -> x0, local copies, waits for them, and re-layouts: 16.7 us -> none  [the longest x1 4.14 us: on_device(): sig_im.astype(jnp.bfloat16)]
  transfers between devices with their start and end apart: 11 -> 10, of which waited for: 8 -> 5; matrix products, arithmetic and copies ran while one was open for 15% -> 0% of each run, Pallas kernels for 0% -> 25%
where the time goes in v2:
time: 83.5 us; the launch traced here: 83 us
  Pallas kernels  32.8 us (39%)
  starting transfers between devices  32.5 us (39%)
  waiting for transfers between devices  16.5 us (20%)
    pallas_call x2, Pallas kernels, local_call(): pl.pallas_call(functools.partial(local_kernel, first), grid=(NH,), in_spe...  15.7 us
    all_to_all x2, waiting for transfers between devices, exchange(): return lax.all_to_all(value, everyone, 0, 0, tiled=True)  15.6 us
    pallas_call x4, Pallas kernels, run(): pl.pallas_call(kernel, in_specs=[VMEM if n in near else HBM for n in rang...  15.4 us
    all_to_all x2, starting transfers between devices, exchange(): return lax.all_to_all(value, everyone, 0, 0, tiled=True)  15.3 us
    ppermute x7, starting transfers between devices, moved(): return lax.ppermute(value, 'ch', [(i, target(i)) for i in range(2 * NH)])  11.4 us
    ppermute x1, starting transfers between devices, on_device(): lax.ppermute(edges, everyone, [(i, i + 1) for i in range(total - 1)])  5.7 us
    pallas_call x1, Pallas kernels, edge_call(): pl.pallas_call(edge_kernel, in_specs=[ANY, ANY, ANY], out_specs=VMEM, out...  1.75 us
  transfers between devices with their start and end apart: 10, of which 5 were waited for; matrix products, arithmetic and copies ran while one was open for 0% of the time, Pallas kernels for 25%

profile of v2, /device:TPU:1, one launch (start us, length us, event | category | flops | bytes accessed | tf_op | source)
XLA Modules:
  0.0 83.0 jit_solution(3754969436018689088)
XLA Ops:
  0.0 0.8 pad_maximum_fusion.refs_0_
  0.8 6.9 %collective-permute-start.2 = (f32[32,512]{1,0:T(8,128)S(1)}, f32[32,512]{1,0:T(8,128)S(1)}, u32[]{:S(2)}, u32[]{:S(2)}) collective-permute-start(f32[32,512]{1,0:T(8,128)S(1)} %pad_maximum_fusion.refs_0_), channel_id=1, source_target_pairs={{0,6},{1,7},{2,0},{3,1},{4,2},{5,3},{6,4},{7,5},{8,14},{9,15},{10,... | collective-permute-start | bytes 196616 | tf_op jit(solution)/shard_map/ppermute | solution.py:474
  7.7 1.0 %collective-permute-start.1 = (f32[32,512]{1,0:T(8,128)S(1)}, f32[32,512]{1,0:T(8,128)S(1)}, u32[]{:S(2)}, u32[]{:S(2)}) collective-permute-start(f32[32,512]{1,0:T(8,128)S(1)} %pad_maximum_fusion.refs_0_), channel_id=1, source_target_pairs={{0,4},{1,5},{2,6},{3,7},{4,0},{5,1},{6,2},{7,3},{8,12},{9,13},{10,... | collective-permute-start | bytes 196616 | tf_op jit(solution)/shard_map/ppermute | solution.py:474
  8.7 1.7 %shard_map.100 = f32[8,4096]{1,0:T(8,128)} custom-call(bf16[128,4096]{1,0:T(8,128)(2,1)} %refs_10_.5, bf16[128,4096]{1,0:T(8,128)(2,1)} %refs_9_.1, bf16[128,4096]{1,0:T(8,128)(2,1)} %refs_10_.3), custom_call_target="tpu_custom_call" | custom-call | flops 1048576 | bytes 1048576 | tf_op jit(solution)/shard_map/pallas_call | solution.py:87
  10.4 2.3 %collective-permute-start = (f32[32,512]{1,0:T(8,128)S(1)}, f32[32,512]{1,0:T(8,128)S(1)}, u32[]{:S(2)}, u32[]{:S(2)}) collective-permute-start(f32[32,512]{1,0:T(8,128)S(1)} %pad_maximum_fusion.refs_0_), channel_id=1, source_target_pairs={{0,2},{1,3},{2,4},{3,5},{4,6},{5,7},{6,0},{7,1},{8,10},{9,11},{10,... | collective-permute-start | bytes 196616 | tf_op jit(solution)/shard_map/ppermute | solution.py:474
  12.8 5.7 %collective-permute-start.7 = (f32[8,4096]{1,0:T(8,128)}, f32[8,4096]{1,0:T(8,128)S(1)}, u32[]{:S(2)}, u32[]{:S(2)}) collective-permute-start(f32[8,4096]{1,0:T(8,128)} %shard_map.100), channel_id=1, source_target_pairs={{0,1},{1,2},{2,3},{3,4},{4,5},{5,6},{6,7},{7,8},{8,9},{9,10},{10,1... | collective-permute-start | bytes 393224 | tf_op jit(solution)/shard_map/ppermute | solution.py:500
  18.5 0.1 collective-permute-start.3
  18.6 3.4 %shard_map.101.refs_8_.refs_11_ = bf16[128,4096]{1,0:T(8,128)(2,1)} custom-call(bf16[128,4096]{1,0:T(8,128)(2,1)} %refs_9_.1, bf16[128,4096]{1,0:T(8,128)(2,1)} %refs_10_.3, f32[3,3,4096]{2,1,0:T(4,128)} %refs_12_.5), custom_call_target="tpu_custom_call" | custom-call | flops 6291456 | bytes 1048576 | tf_op jit(solution)/shard_map/pallas_call | solution.py:157
  22.0 0.0 collective-permute-done.2.refs_3_
  22.0 0.0 copy-start.2
  22.0 0.0 collective-permute-done.1.refs_2_
  22.0 0.0 copy-start.3
  22.0 0.0 collective-permute-done.refs_1_
  22.0 0.0 copy-start.4
  22.0 0.6 collective-permute-start.4
  22.6 0.1 collective-permute-start.5
  22.7 0.4 collective-permute-start.6
  23.1 0.0 collective-permute-done.3.refs_4_
  23.1 0.0 collective-permute-done.7.refs_11_
  23.1 0.0 copy-start.1
  23.1 0.4 collective-permute-done.4.refs_5_
  23.5 0.3 collective-permute-done.5.refs_6_
  23.9 0.2 collective-permute-done.6.refs_7_
  24.0 4.8 %shard_map.102 = (f32[512,128]{1,0:T(8,128)}, bf16[16,4096]{1,0:T(8,128)(2,1)}, f32[8,128]{1,0:T(8,128)S(1)}) custom-call(f32[32,512]{1,0:T(8,128)S(1)} %pad_maximum_fusion.refs_0_, f32[32,512]{1,0:T(8,128)S(1)} %collective-permute-done.refs_1_, f32[32,512]{1,0:T(8,128)S(1)} %collective-permute-done.1.refs_2_, f32[32,512]{1,0:T(8,128)S(1)} %collective-permute-done.2.refs_3_, ...), custom_call_target="tpu_custom_call" | custom-call | flops 16777216 | bytes 1048576 | tf_op jit(solution)/shard_map/pallas_call | solution.py:157
  28.9 9.4 %all-to-all-start = ((f32[256,2,128]{2,1,0:T(2,128)}), f32[256,2,128]{2,1,0:T(2,128)S(1)}, u32[]{:S(2)}, u32[]{:S(2)}) async-start(f32[256,2,128]{2,1,0:T(2,128)} %bitcast.2), calls=%async_computation | async-start | bytes 524288 | tf_op jit(solution)/shard_map/all_to_all | solution.py:508
  38.3 7.9 %shard_map.103 = (f32[128,2048]{1,0:T(8,128)}, bf16[128,2048]{1,0:T(8,128)(2,1)}) custom-call(f32[32,512]{1,0:T(8,128)} %copy-done, f32[32,512]{1,0:T(8,128)} %copy-done.4, f32[32,512]{1,0:T(8,128)} %copy-done.3, f32[32,512]{1,0:T(8,128)} %copy-done.2, f32[32,512]{1,0:T(8,128)} %copy-done.5, f32[32,512]{1,0:T(8,128)} %copy-done.6, f32[32,512]{1,0:T(8,128)} %copy-done.7, ...), custom_call_target="tpu_custom_call" | custom-call | flops 536870912 | bytes 1048576 | tf_op jit(solution)/shard_map/pallas_call | solution.py:369
  46.2 7.8 %all-to-all-done.got_ref = f32[256,2,128]{2,1,0:T(2,128)S(1)} async-done(((f32[256,2,128]{2,1,0:T(2,128)}), f32[256,2,128]{2,1,0:T(2,128)S(1)}, u32[]{:S(2)}, u32[]{:S(2)}) %all-to-all-start) | async-done | bytes 262176 | tf_op jit(solution)/shard_map/all_to_all | solution.py:508
  54.0 1.2 %shard_map.104 = f32[256,2,128]{2,1,0:T(2,128)} custom-call(f32[256,2,128]{2,1,0:T(2,128)S(1)} %all-to-all-done.got_ref, f32[8,128]{1,0:T(8,128)S(1)} %get-tuple-element.31.decay_ref), custom_call_target="tpu_custom_call" | custom-call | flops 131072 | bytes 1048576 | tf_op jit(solution)/shard_map/pallas_call | solution.py:157
  55.2 5.9 %all-to-all-start.1 = ((f32[256,2,128]{2,1,0:T(2,128)}), f32[256,2,128]{2,1,0:T(2,128)S(1)}, u32[]{:S(2)}, u32[]{:S(2)}) async-start(f32[256,2,128]{2,1,0:T(2,128)} %shard_map.104), calls=%async_computation.1 | async-start | bytes 524288 | tf_op jit(solution)/shard_map/all_to_all | solution.py:508
  61.2 7.9 %shard_map.105 = (f32[128,2048]{1,0:T(8,128)}, bf16[128,2048]{1,0:T(8,128)(2,1)}) custom-call(f32[32,512]{1,0:T(8,128)} %copy-done, f32[32,512]{1,0:T(8,128)} %copy-done.4, f32[32,512]{1,0:T(8,128)} %copy-done.3, f32[32,512]{1,0:T(8,128)} %copy-done.2, f32[32,512]{1,0:T(8,128)} %copy-done.5, f32[32,512]{1,0:T(8,128)} %copy-done.6, f32[32,512]{1,0:T(8,128)} %copy-done.7, ...), custom_call_target="tpu_custom_call" | custom-call | flops 536870912 | bytes 1048576 | tf_op jit(solution)/shard_map/pallas_call | solution.py:369
  69.0 7.8 %all-to-all-done.1 = f32[256,2,128]{2,1,0:T(2,128)S(1)} async-done(((f32[256,2,128]{2,1,0:T(2,128)}), f32[256,2,128]{2,1,0:T(2,128)S(1)}, u32[]{:S(2)}, u32[]{:S(2)}) %all-to-all-start.1) | async-done | bytes 262176 | tf_op jit(solution)/shard_map/all_to_all | solution.py:508
  76.9 6.0 %shard_map.106 = bf16[128,4096]{1,0:T(8,128)(2,1)} custom-call(f32[32,512]{1,0:T(8,128)} %copy-done, f32[32,512]{1,0:T(8,128)} %copy-done.4, f32[32,512]{1,0:T(8,128)} %copy-done.3, f32[32,512]{1,0:T(8,128)} %copy-done.2, f32[32,512]{1,0:T(8,128)} %copy-done.5, f32[32,512]{1,0:T(8,128)} %copy-done.6, f32[32,512]{1,0:T(8,128)} %copy-done.7, ...), custom_call_target="tpu_custom_call" | custom-call | flops 16777216 | bytes 1048576 | tf_op jit(solution)/shard_map/pallas_call | solution.py:157
  (14 shorter events, 0.0 us)
Async XLA Ops:
  0.8 23.2 %copy-start = (f32[32,512]{1,0:T(8,128)}, f32[32,512]{1,0:T(8,128)S(1)}, u32[]{:S(2)}) copy-start(f32[32,512]{1,0:T(8,128)S(1)} %pad_maximum_fusion.refs_0_) | copy-start | bytes 196612
  0.8 21.2 %collective-permute-start.2 = (f32[32,512]{1,0:T(8,128)S(1)}, f32[32,512]{1,0:T(8,128)S(1)}, u32[]{:S(2)}, u32[]{:S(2)}) collective-permute-start(f32[32,512]{1,0:T(8,128)S(1)} %pad_maximum_fusion.refs_0_), channel_id=1, source_target_pairs={{0,6},{1,7},{2,0},{3,1},{4,2},{5,3},{6,4},{7,5},{8,14},{9,15},{10,... | collective-permute-start | bytes 196616 | tf_op jit(solution)/shard_map/ppermute | solution.py:474
  7.7 14.3 %collective-permute-start.1 = (f32[32,512]{1,0:T(8,128)S(1)}, f32[32,512]{1,0:T(8,128)S(1)}, u32[]{:S(2)}, u32[]{:S(2)}) collective-permute-start(f32[32,512]{1,0:T(8,128)S(1)} %pad_maximum_fusion.refs_0_), channel_id=1, source_target_pairs={{0,4},{1,5},{2,6},{3,7},{4,0},{5,1},{6,2},{7,3},{8,12},{9,13},{10,... | collective-permute-start | bytes 196616 | tf_op jit(solution)/shard_map/ppermute | solution.py:474
  10.4 11.6 %collective-permute-start = (f32[32,512]{1,0:T(8,128)S(1)}, f32[32,512]{1,0:T(8,128)S(1)}, u32[]{:S(2)}, u32[]{:S(2)}) collective-permute-start(f32[32,512]{1,0:T(8,128)S(1)} %pad_maximum_fusion.refs_0_), channel_id=1, source_target_pairs={{0,2},{1,3},{2,4},{3,5},{4,6},{5,7},{6,0},{7,1},{8,10},{9,11},{10,... | collective-permute-start | bytes 196616 | tf_op jit(solution)/shard_map/ppermute | solution.py:474
  12.8 10.3 %collective-permute-start.7 = (f32[8,4096]{1,0:T(8,128)}, f32[8,4096]{1,0:T(8,128)S(1)}, u32[]{:S(2)}, u32[]{:S(2)}) collective-permute-start(f32[8,4096]{1,0:T(8,128)} %shard_map.100), channel_id=1, source_target_pairs={{0,1},{1,2},{2,3},{3,4},{4,5},{5,6},{6,7},{7,8},{8,9},{9,10},{10,1... | collective-permute-start | bytes 393224 | tf_op jit(solution)/shard_map/ppermute | solution.py:500
  18.5 4.6 %collective-permute-start.3 = (f32[32,512]{1,0:T(8,128)S(1)}, f32[32,512]{1,0:T(8,128)S(1)}, u32[]{:S(2)}, u32[]{:S(2)}) collective-permute-start(f32[32,512]{1,0:T(8,128)S(1)} %pad_maximum_fusion.refs_0_), channel_id=1, source_target_pairs={{0,1},{1,0},{2,3},{3,2},{4,5},{5,4},{6,7},{7,6},{8,9},{9,8},{10,11... | collective-permute-start | bytes 196616 | tf_op jit(solution)/shard_map/ppermute | solution.py:474
  22.0 6.9 %copy-start.2 = (f32[32,512]{1,0:T(8,128)}, f32[32,512]{1,0:T(8,128)S(1)}, u32[]{:S(2)}) copy-start(f32[32,512]{1,0:T(8,128)S(1)} %collective-permute-done.2.refs_3_) | copy-start | bytes 196612
  22.0 6.8 %copy-start.3 = (f32[32,512]{1,0:T(8,128)}, f32[32,512]{1,0:T(8,128)S(1)}, u32[]{:S(2)}) copy-start(f32[32,512]{1,0:T(8,128)S(1)} %collective-permute-done.1.refs_2_) | copy-start | bytes 196612
  22.0 6.8 %copy-start.4 = (f32[32,512]{1,0:T(8,128)}, f32[32,512]{1,0:T(8,128)S(1)}, u32[]{:S(2)}) copy-start(f32[32,512]{1,0:T(8,128)S(1)} %collective-permute-done.refs_1_) | copy-start | bytes 196612
  22.0 1.5 %collective-permute-start.4 = (f32[32,512]{1,0:T(8,128)S(1)}, f32[32,512]{1,0:T(8,128)S(1)}, u32[]{:S(2)}, u32[]{:S(2)}) collective-permute-start(f32[32,512]{1,0:T(8,128)S(1)} %collective-permute-done.refs_1_), channel_id=1, source_target_pairs={{0,1},{1,0},{2,3},{3,2},{4,5},{5,4},{6,7},{7,6},{8,9},{9,8},{10,11... | collective-permute-start | bytes 196616 | tf_op jit(solution)/shard_map/ppermute | solution.py:474
  22.6 1.3 %collective-permute-start.5 = (f32[32,512]{1,0:T(8,128)S(1)}, f32[32,512]{1,0:T(8,128)S(1)}, u32[]{:S(2)}, u32[]{:S(2)}) collective-permute-start(f32[32,512]{1,0:T(8,128)S(1)} %collective-permute-done.1.refs_2_), channel_id=1, source_target_pairs={{0,1},{1,0},{2,3},{3,2},{4,5},{5,4},{6,7},{7,6},{8,9},{9,8},{10,11... | collective-permute-start | bytes 196616 | tf_op jit(solution)/shard_map/ppermute | solution.py:474
  22.7 1.3 %collective-permute-start.6 = (f32[32,512]{1,0:T(8,128)S(1)}, f32[32,512]{1,0:T(8,128)S(1)}, u32[]{:S(2)}, u32[]{:S(2)}) collective-permute-start(f32[32,512]{1,0:T(8,128)S(1)} %collective-permute-done.2.refs_3_), channel_id=1, source_target_pairs={{0,1},{1,0},{2,3},{3,2},{4,5},{5,4},{6,7},{7,6},{8,9},{9,8},{10,11... | collective-permute-start | bytes 196616 | tf_op jit(solution)/shard_map/ppermute | solution.py:474
  23.1 5.7 %copy-start.5 = (f32[32,512]{1,0:T(8,128)}, f32[32,512]{1,0:T(8,128)S(1)}, u32[]{:S(2)}) copy-start(f32[32,512]{1,0:T(8,128)S(1)} %collective-permute-done.3.refs_4_) | copy-start | bytes 196612
  23.1 5.7 %copy-start.1 = (f32[8,4096]{1,0:T(8,128)}, f32[8,4096]{1,0:T(8,128)S(1)}, u32[]{:S(2)}) copy-start(f32[8,4096]{1,0:T(8,128)S(1)} %collective-permute-done.7.refs_11_) | copy-start | bytes 393220
  23.5 5.4 %copy-start.6 = (f32[32,512]{1,0:T(8,128)}, f32[32,512]{1,0:T(8,128)S(1)}, u32[]{:S(2)}) copy-start(f32[32,512]{1,0:T(8,128)S(1)} %collective-permute-done.4.refs_5_) | copy-start | bytes 196612
  23.9 5.0 %copy-start.7 = (f32[32,512]{1,0:T(8,128)}, f32[32,512]{1,0:T(8,128)S(1)}, u32[]{:S(2)}) copy-start(f32[32,512]{1,0:T(8,128)S(1)} %collective-permute-done.5.refs_6_) | copy-start | bytes 196612
  24.0 4.9 %copy-start.8 = (f32[32,512]{1,0:T(8,128)}, f32[32,512]{1,0:T(8,128)S(1)}, u32[]{:S(2)}) copy-start(f32[32,512]{1,0:T(8,128)S(1)} %collective-permute-done.6.refs_7_) | copy-start | bytes 196612
  28.9 25.1 %all-to-all-start = ((f32[256,2,128]{2,1,0:T(2,128)}), f32[256,2,128]{2,1,0:T(2,128)S(1)}, u32[]{:S(2)}, u32[]{:S(2)}) async-start(f32[256,2,128]{2,1,0:T(2,128)} %bitcast.2), calls=%async_computation | async-start | bytes 524288 | tf_op jit(solution)/shard_map/all_to_all | solution.py:508
  55.2 21.6 %all-to-all-start.1 = ((f32[256,2,128]{2,1,0:T(2,128)}), f32[256,2,128]{2,1,0:T(2,128)S(1)}, u32[]{:S(2)}, u32[]{:S(2)}) async-start(f32[256,2,128]{2,1,0:T(2,128)} %shard_map.104), calls=%async_computation.1 | async-start | bytes 524288 | tf_op jit(solution)/shard_map/all_to_all | solution.py:508

commit v3 on v2

--- a/solution.py
+++ b/solution.py
@@ -76,10 +76,8 @@
     ]
     for copy in copies:
         copy.wait()
-    for at in range(0, edge_ref.shape[1], 512):
-        lanes = slice(at, at + 512)
-        two = [last[n, :, lanes].astype(F32)[14:] for n in range(3)]
-        edge_ref[:, lanes] = jnp.concatenate(two + [two[0]], axis=0)
+    for n in range(3):
+        edge_ref[n] = last[n, 14:16, :]
 
 
 def edge_call(q_proj, k_proj, v_proj):
@@ -88,7 +86,7 @@
         edge_kernel,
         in_specs=[ANY, ANY, ANY],
         out_specs=VMEM,
-        out_shape=jax.ShapeDtypeStruct((8, width), F32),
+        out_shape=jax.ShapeDtypeStruct((3, 2, width), BF16),
         scratch_shapes=[pltpu.VMEM((3, 16, width), BF16), pltpu.SemaphoreType.DMA((3,))],
         compiler_params=GRANT,
         cost_estimate=cost(1 << 20),
@@ -228,8 +226,8 @@
 
 
 def state_kernel(*refs):
-    pars, (sig_any, k_any, v_any, edge, filt_any, state, top_any, decay) = refs[: 2 * NH], refs[2 * NH : 2 * NH + 8]
-    par0, par1, packed, k_top, v_top, filt, sig, top, sems = refs[2 * NH + 8 :]
+    pars, (sig_any, k_any, v_any, edge, filt_any, state_out, top_any, decay, edge_any) = refs[: 2 * NH], refs[2 * NH : 2 * NH + 9]
+    par0, par1, packed, k_top, v_top, filt, sig, top, state, sems = refs[2 * NH + 9 :]
     place = where_am_i()
     mover = Mover(sems)
     modes, group = par0.shape[1] // 2, par0.shape[2]
@@ -244,13 +242,14 @@
         (par0, par1)[n // NH][n % NH] = array[...]
     parts = [slice(at, at + group) for at in range(0, width, group)]
     signals = [mover.start(sig_any.at[:, at], packed.at[:, at]) for at in parts]
+    kept = mover.start(edge, edge_any)
     for copy in small:
         copy.wait()
     for n, at in enumerate(parts):
         signals[n].wait()
         sig[...] = packed[:, at].astype(F32)
-        key = mix_top(k_top[:, at].astype(F32), edge[2:4, at], filt[0, :, at])
-        value = mix_top(v_top[:, at].astype(F32), edge[4:6, at], filt[1, :, at])
+        key = mix_top(k_top[:, at].astype(F32), edge[1, :, at].astype(F32), filt[0, :, at])
+        value = mix_top(v_top[:, at].astype(F32), edge[2, :, at].astype(F32), filt[1, :, at])
         s0, s1 = rounded(key[0] * value[0]), rounded(key[1] * value[1])
         top[:, at] = top_rows(s0, s1, sig[0:16, :]).astype(BF16)
         rates = params_of(place, n // 2, n % 2, par0, par1, slice(0, modes))
@@ -260,7 +259,9 @@
             state[pl.ds(base + j, modes, stride=blocks), :] = value[:, j * LANE : (j + 1) * LANE]
     sent = mover.start(top, top_any)
     decay[...] = own_decay(place, par0, par1, float(sig.shape[0]))
+    state_out[...] = state[...].astype(BF16)
     sent.wait()
+    kept.wait()
 
 
 def state_call(pars, sig, k_proj, v_proj, edges, filt):
@@ -271,35 +272,36 @@
     return run(
         state_kernel,
         *pars, sig, k_proj, v_proj, edges, filt,
-        out=[((count, LANE), F32), ((16, width), BF16), ((8, LANE), F32)],
+        out=[((count, LANE), BF16), ((16, width), BF16), ((8, LANE), F32), (edges.shape, BF16)],
         scratch=[
             par, par, ((rows, width), BF16), ((16, width), BF16), ((16, width), BF16),
-            ((2, 3, width), F32), ((rows, group), F32), ((16, width), BF16),
+            ((2, 3, width), F32), ((rows, group), F32), ((16, width), BF16), ((count, LANE), F32),
         ],
         near=[*range(2 * NH), 2 * NH + 3],
         near_out=[0, 2],
-        copies=4 + width // group,
+        copies=5 + width // group,
         flops=rows * width * modes * 2,
     )
 
 
-def scan_kernel(got_ref, decay_ref, out_ref, _):
+def scan_kernel(got_ref, decay_ref, out_ref, got, sent, _):
+    got[...] = got_ref[...].astype(F32)
     decay = decay_ref[0:2, :]
     total = jnp.zeros((2, LANE), F32)
-    for n in range(got_ref.shape[0]):
-        out_ref[n] = total
-        total = total * decay + got_ref[n]
+    for n in range(0, got.shape[0], 2):
+        sent[n : n + 2, :] = total
+        total = total * decay + got[n : n + 2, :]
+    out_ref[...] = sent[...].astype(BF16)
 
 
 def scan_call(got, decay):
-    return run(scan_kernel, got, decay, out=[(got.shape, F32)], near=[0, 1], near_out=[0], flops=got.size * 2)[0]
-
-
-def decaying_sum(start_ref, rate_ref, step_ref, at, first, store, rows):
-    modes = start_ref.shape[0]
-    ramp = lax.broadcasted_iota(jnp.int32, (8, LANE), 0).astype(F32) + first
-    terms = [start_ref[m : m + 1, at] * jnp.exp(-rate_ref[m : m + 1, at] * ramp) for m in range(modes)]
-    steps = [jnp.broadcast_to(step_ref[m : m + 1, at], (8, LANE)) for m in range(modes)]
+    return run(
+        scan_kernel, got, decay,
+        out=[(got.shape, BF16)], scratch=[(got.shape, F32)] * 2, near=[0, 1], near_out=[0], flops=got.size * 2,
+    )[0]
+
+
+def decaying_sum(terms, steps, store, rows):
     for tile in range(rows // 8):
         total = terms
         while len(total) > 1:
@@ -310,8 +312,9 @@
 
 
 def local_kernel(first, *refs):
-    sig_ref, top_ref, q_ref, edge_ref, filt_ref, fwd_ref, inv_ref, shift_ref, conv_ref, query_ref = refs[2 * NH : 2 * NH + 10]
-    par0, par1, taps_ref, rate_s, step_s, weight_s, sems = refs[2 * NH + 10 :]
+    sig_ref, top_ref, q_ref, edge_ref, filt_ref, fwd_ref, inv_ref, shift_ref = refs[2 * NH : 2 * NH + 8]
+    conv_ref, query_ref, term_ref, step_s = refs[2 * NH + 8 : 2 * NH + 12]
+    par0, par1, taps_ref, rate_s, decay_s, weight_s, sems = refs[2 * NH + 12 :]
     place = where_am_i()
     rows, group = sig_ref.shape
     modes = par0.shape[1] // 2
@@ -328,14 +331,22 @@
         rate_s[...], params_of(place, chip, parity, par0, par1, slice(modes, 2 * modes))
     )
     step_s[...] = jnp.exp(-8.0 * rate_s[...])
+    decay_s[...] = jnp.exp(-rate_s[...])
+    ramp = lax.broadcasted_iota(jnp.int32, (8, LANE), 0).astype(F32)
 
     def body(n, _):
         lanes = pl.ds(pl.multiple_of(n * LANE, LANE), LANE)
+        terms = []
+        for m in range(modes):
+            one = slice(m, m + 1)
+            terms.append(weight_s[one, lanes] * jnp.exp(-rate_s[one, lanes] * ramp))
+            term_ref[8 * m : 8 * m + 8, lanes] = terms[m] * decay_s[one, lanes]
 
         def store(tile, value):
             taps_ref[tile, lanes] = value
 
-        decaying_sum(weight_s, rate_s, step_s, lanes, 0.0, store, rows)
+        steps = [jnp.broadcast_to(step_s[m : m + 1, lanes], (8, LANE)) for m in range(modes)]
+        decaying_sum(terms, steps, store, rows)
         return 0
 
     lax.fori_loop(0, group // LANE, body, 0)
@@ -349,7 +360,7 @@
         inv_ref[...], jnp.concatenate([ph, ph, pw], axis=0), preferred_element_type=F32
     )
     query = mix_shifted(shift_ref[...], q_ref[...], filt_ref[0])
-    q0, q1 = mix_top(q_ref[0:16, :].astype(F32), edge_ref[0:2, :], filt_ref[0])
+    q0, q1 = mix_top(q_ref[0:16, :].astype(F32), edge_ref[0].astype(F32), filt_ref[0])
     query_ref[...] = top_rows(q0, q1, query).astype(BF16)
 
 
@@ -371,13 +382,15 @@
         grid=(NH,),
         in_specs=[ANY] * (2 * NH) + [
             pl.BlockSpec((rows, group), lanes), pl.BlockSpec((16, group), lanes), pl.BlockSpec((rows, group), lanes),
-            pl.BlockSpec((8, group), lanes), pl.BlockSpec((3, 3, group), lambda n: (0, 0, n + first)),
+            pl.BlockSpec((3, 2, group), lambda n: (0, 0, n + first)), pl.BlockSpec((3, 3, group), lambda n: (0, 0, n + first)),
             whole(fwd), whole(inv), whole(shift),
         ],
-        out_specs=[block, block],
+        out_specs=[block, block] + [pl.BlockSpec((count, group), lambda n: (0, n)) for count in (8 * modes, modes)],
         out_shape=[
             jax.ShapeDtypeStruct((rows, width // 2), F32),
             jax.ShapeDtypeStruct((rows, width // 2), BF16),
+            jax.ShapeDtypeStruct((8 * modes, width // 2), F32),
+            jax.ShapeDtypeStruct((modes, width // 2), F32),
         ],
         scratch_shapes=[par, par, pltpu.VMEM((rows, group), F32)]
         + [pltpu.VMEM((modes, group), F32)] * 3 + [pltpu.SemaphoreType.DMA((2 * NH,))],
@@ -386,50 +399,33 @@
     )(*pars, sig, top, q_proj, edges, filt, fwd, inv, shift)
 
 
-def carry_kernel(*refs):
-    pars, (state, top_any, skip_any, sig_any) = refs[: 2 * NH], refs[2 * NH : 2 * NH + 4]
-    conv_anys, query_anys = refs[2 * NH + 4 : 2 * NH + 6], refs[2 * NH + 6 : 2 * NH + 8]
-    out_any, par0, par1, sig, top, skip, conv, query, out, start_s, step_s, rate_s, sems = refs[2 * NH + 8 :]
-    place = where_am_i()
+def carry_kernel(state_ref, top_any, skip_any, sig_any, *refs):
+    conv_anys, query_anys, term_anys, step_anys = (refs[2 * n : 2 * n + 2] for n in range(4))
+    out_any, sig, top, skip, conv, query, term, step, out, state, sems = refs[8:]
     mover = Mover(sems)
     rows, width = sig.shape
-    modes, group = par0.shape[1] // 2, par0.shape[2]
-    blocks = group // LANE
-    small = [
-        *fetch_params(mover, pars, par0, par1),
-        mover.start(top_any, top),
-        mover.start(skip_any, skip),
-    ]
-    span = width // 2
+    modes = step.shape[0]
+    group = 512
+    blocks, span = group // LANE, width // 2
     parts = [slice(at, at + group) for at in range(0, width, group)]
     fetched = []
     for at in parts:
         n, inside = at.start // span, slice(at.start % span, at.start % span + group)
-        fetched.append(
-            [
-                mover.start(conv_anys[n].at[:, inside], conv.at[:, at]),
-                mover.start(query_anys[n].at[:, inside], query.at[:, at]),
-                mover.start(sig_any.at[:, at], sig.at[:, at]),
-            ]
-        )
-    for copy in small:
-        copy.wait()
+        copies = [
+            mover.start(anys[n].at[:, inside], here.at[:, at])
+            for anys, here in ((step_anys, step), (term_anys, term), (conv_anys, conv), (query_anys, query))
+        ]
+        copies.append(mover.start(sig_any.at[:, at], sig.at[:, at]))
+        if at.start == 0:
+            copies += [mover.start(top_any, top), mover.start(skip_any, skip)]
+        fetched.append(copies)
+    state[...] = state_ref[...].astype(F32)
     sent = []
     for n, at in enumerate(parts):
-        rate_s[...] = params_of(place, n // 2, n % 2, par0, par1, slice(0, modes))
-        step_s[...] = jnp.exp(-8.0 * rate_s[...])
-        weights = weights_of(
-            rate_s[...], params_of(place, n // 2, n % 2, par0, par1, slice(modes, 2 * modes))
-        )
-        for j in range(blocks):
-            lanes = slice(j * LANE, (j + 1) * LANE)
-            from_state = state[pl.ds(n * modes * blocks + j, modes, stride=blocks), :]
-            start_s[:, lanes] = weights[:, lanes] * from_state
         for copy in fetched[n]:
             copy.wait()
 
         def body(j, _):
-            lanes = pl.ds(pl.multiple_of(j * LANE, LANE), LANE)
             here = pl.ds(pl.multiple_of(at.start + j * LANE, LANE), LANE)
             direct = skip[:, here]
             held = []
@@ -443,7 +439,12 @@
                     out[both, here] = (query[both, here].astype(F32) * total).astype(BF16)
                     held.clear()
 
-            decaying_sum(start_s, rate_s, step_s, lanes, 1.0, store, rows)
+            terms = [
+                term[8 * m : 8 * m + 8, here] * state[pl.ds((n * modes + m) * blocks + j, 1), :]
+                for m in range(modes)
+            ]
+            steps = [jnp.broadcast_to(step[m : m + 1, here], (8, LANE)) for m in range(modes)]
+            decaying_sum(terms, steps, store, rows)
             return 0
 
         lax.fori_loop(0, blocks, body, 0)
@@ -452,20 +453,19 @@
         copy.wait()
 
 
-def carry_call(pars, states, top, skip, sig, convs, queries):
+def carry_call(states, top, skip, sig, convs, queries, terms, steps):
     rows, width = sig.shape
-    modes, group = pars[0].shape[0] // 2, pars[0].shape[1]
-    par, half = ((NH, 2 * modes, group), F32), ((rows, width), BF16)
+    half, modes = ((rows, width), BF16), steps[0].shape[0]
     return run(
         carry_kernel,
-        *pars, states, top, skip, sig, *convs, *queries,
+        states, top, skip, sig, *convs, *queries, *terms, *steps,
         out=[half],
         scratch=[
-            par, par, half, (top.shape, BF16), (skip.shape, F32),
-            ((rows, width), F32), half, half,
-        ] + [((modes, group), F32)] * 3,
-        near=[2 * NH],
-        copies=2 + 2 * NH + 4 * (width // group),
+            half, (top.shape, BF16), (skip.shape, F32), ((rows, width), F32), half,
+            ((8 * modes, width), F32), ((modes, width), F32), half, (states.shape, F32),
+        ],
+        near=[0],
+        copies=2 + 6 * (width // 512),
         flops=rows * width * modes * 2,
     )[0]
 
@@ -476,6 +476,16 @@
 
 def to_chip(value, by):
     return moved(value, lambda i: (i + 2 * by) % (2 * NH))
+
+
+def to_far(value):
+    count, ring = lax.axis_size("seq"), 2 * NH
+    pairs = [
+        (s * ring + c, (s + count // 2) % count * ring + (c + NH) % ring)
+        for s in range(count)
+        for c in range(ring)
+    ]
+    return lax.ppermute(value, ("seq", "ch"), pairs)
 
 
 def to_core(value):
@@ -494,15 +504,16 @@
     shift = jnp.asarray(shifts(rows))
 
     own = jnp.concatenate([rates.T, residues.T], axis=0)
-    far = to_chip(own, 2)
+    far = to_far(own)
     edges = edge_call(q_proj, k_proj, v_proj)
     one = to_chip(after(own, edges), 1)
-    edges = lax.ppermute(edges, everyone, [(i, i + 1) for i in range(total - 1)])
+    last = lax.ppermute(edges, everyone, [(i, i + 2) for i in range(1, total - 2, 2)])
+    edges = to_core(jnp.where(lax.axis_index("ch") % 2 == 1, last, edges))
     three = to_chip(own, 3)
     sig = signal_call(k_proj, v_proj, short_filter)
     mine = [own, one, far, three]
     pars = mine + [to_core(own)] + [to_core(after(value, sig)) for value in mine[1:]]
-    states, top, decay = state_call(pars, sig, k_proj, v_proj, edges, short_filter)
+    states, top, decay, edges = state_call(pars, sig, k_proj, v_proj, edges, short_filter)
 
     def exchange(value):
         return lax.all_to_all(value, everyone, 0, 0, tiled=True)
@@ -510,12 +521,11 @@
     def local(half):
         return local_call(half, pars, sig, top, q_proj, edges, short_filter, fwd, inv, shift)
 
-    got = exchange(states.reshape(total, -1, LANE))
+    got = exchange(states.reshape(total, -1, LANE)).reshape(states.shape)
     got, *early = lax.optimization_barrier((got, *local(0)))
-    carry = exchange(scan_call(got, decay))
+    carry = exchange(scan_call(got, decay).reshape(total, -1, LANE)).reshape(states.shape)
     carry, *late = lax.optimization_barrier((carry, *local(1)))
-    convs, queries = zip(early, late)
-    return carry_call(pars, carry.reshape(states.shape), top, skip[None, :], sig, convs, queries)
+    return carry_call(carry, top, skip[None, :], sig, *zip(early, late))
 
 
 def solution(mesh):

time: 83.5 us -> 80 us (0.958)
  waiting for transfers between devices: 16.5 us -> 10.6 us
  starting transfers between devices: 32.5 us -> 34.3 us
    all_to_all x2, waiting for transfers between devices: 15.6 us -> 9.44 us  [exchange(): return lax.all_to_all(value, everyone, 0, 0, tiled=True)]
    all_to_all x2, starting transfers between devices: 15.3 us -> 18.8 us  [exchange(): return lax.all_to_all(value, everyone, 0, 0, tiled=True)]
    ppermute x7, starting transfers between devices: 11.4 us -> 10.4 us  [moved(): return lax.ppermute(value, 'ch', [(i, target(i)) for i in range(2 * NH)])]
    ppermute x1 -> x2, starting transfers between devices: 5.7 us -> 5.01 us  [the longest x1 4.3 us: on_device(): lax.ppermute(edges, everyone, [(i, i + 2) for i in range(1, total - 2, 2)])]
  transfers between devices with their start and end apart: 10 -> 11, of which waited for: 5 -> 3; matrix products, arithmetic and copies ran while one was open for 0% -> 0% of each run, Pallas kernels for 25% -> 27%
where the time goes in v3:
time: 80 us; the launch traced here: 79.5 us
  starting transfers between devices  34.3 us (43%)
  Pallas kernels  32.8 us (41%)
  waiting for transfers between devices  10.6 us (13%)
  other arithmetic  0.83 us (1%)
    all_to_all x2, starting transfers between devices, exchange(): return lax.all_to_all(value, everyone, 0, 0, tiled=True)  18.8 us
    pallas_call x2, Pallas kernels, local_call(): pl.pallas_call(functools.partial(local_kernel, first), grid=(NH,), in_spe...  16.1 us
    pallas_call x4, Pallas kernels, run(): pl.pallas_call(kernel, in_specs=[VMEM if n in near else HBM for n in rang...  15 us
    ppermute x7, starting transfers between devices, moved(): return lax.ppermute(value, 'ch', [(i, target(i)) for i in range(2 * NH)])  10.4 us
    all_to_all x2, waiting for transfers between devices, exchange(): return lax.all_to_all(value, everyone, 0, 0, tiled=True)  9.44 us
    ppermute x1, starting transfers between devices, on_device(): lax.ppermute(edges, everyone, [(i, i + 2) for i in range(1, total - 2, 2)])  4.3 us
    pallas_call x1, Pallas kernels, edge_call(): pl.pallas_call(edge_kernel, in_specs=[ANY, ANY, ANY], out_specs=VMEM, out...  1.7 us
  transfers between devices with their start and end apart: 11, of which 3 were waited for; matrix products, arithmetic and copies ran while one was open for 0% of the time, Pallas kernels for 27%

profile of v3, /device:TPU:1, one launch (start us, length us, event | category | flops | bytes accessed | tf_op | source)
XLA Modules:
  0.0 79.5 jit_solution(4214841448875489801)
XLA Ops:
  0.0 0.8 pad_maximum_fusion.refs_0_
  0.8 6.9 %collective-permute-start.2 = (f32[32,512]{1,0:T(8,128)S(1)}, f32[32,512]{1,0:T(8,128)S(1)}, u32[]{:S(2)}, u32[]{:S(2)}) collective-permute-start(f32[32,512]{1,0:T(8,128)S(1)} %pad_maximum_fusion.refs_0_), channel_id=1, source_target_pairs={{0,6},{1,7},{2,0},{3,1},{4,2},{5,3},{6,4},{7,5},{8,14},{9,15},{10,... | collective-permute-start | bytes 196616 | tf_op jit(solution)/shard_map/ppermute | solution.py:474
  7.7 0.7 collective-permute-start.1
  8.4 1.7 %shard_map.100 = bf16[3,2,4096]{2,1,0:T(2,128)(2,1)} custom-call(bf16[128,4096]{1,0:T(8,128)(2,1)} %refs_10_.5, bf16[128,4096]{1,0:T(8,128)(2,1)} %refs_9_.1, bf16[128,4096]{1,0:T(8,128)(2,1)} %refs_10_.3), custom_call_target="tpu_custom_call" | custom-call | flops 1048576 | bytes 1048576 | tf_op jit(solution)/shard_map/pallas_call | solution.py:85
  10.1 2.2 %collective-permute-start = (f32[32,512]{1,0:T(8,128)S(1)}, f32[32,512]{1,0:T(8,128)S(1)}, u32[]{:S(2)}, u32[]{:S(2)}) collective-permute-start(f32[32,512]{1,0:T(8,128)S(1)} %pad_maximum_fusion.refs_0_), channel_id=1, source_target_pairs={{0,2},{1,3},{2,4},{3,5},{4,6},{5,7},{6,0},{7,1},{8,10},{9,11},{10,... | collective-permute-start | bytes 196616 | tf_op jit(solution)/shard_map/ppermute | solution.py:474
  12.3 4.3 %collective-permute-start.7 = (bf16[3,2,4096]{2,1,0:T(2,128)(2,1)}, bf16[3,2,4096]{2,1,0:T(2,128)(2,1)S(1)}, u32[]{:S(2)}, u32[]{:S(2)}) collective-permute-start(bf16[3,2,4096]{2,1,0:T(2,128)(2,1)} %shard_map.100), channel_id=1, source_target_pairs={{1,3},{3,5},{5,7},{7,9},{9,11},{11,13},{13,15},{15,17},{17,19},{19... | collective-permute-start | bytes 147464 | tf_op jit(solution)/shard_map/ppermute | solution.py:510
  16.6 0.1 collective-permute-start.3
  16.7 0.0 copy-start.8
  16.7 3.4 %shard_map.101.refs_8_.sig_any = bf16[128,4096]{1,0:T(8,128)(2,1)} custom-call(bf16[128,4096]{1,0:T(8,128)(2,1)} %refs_9_.1, bf16[128,4096]{1,0:T(8,128)(2,1)} %refs_10_.3, f32[3,3,4096]{2,1,0:T(4,128)} %refs_12_.5), custom_call_target="tpu_custom_call" | custom-call | flops 6291456 | bytes 1048576 | tf_op jit(solution)/shard_map/pallas_call | solution.py:155
  20.1 0.0 collective-permute-done.2.refs_3_
  20.2 0.0 collective-permute-done.1.refs_2_
  20.2 0.0 collective-permute-done.refs_1_
  20.2 0.5 collective-permute-start.4
  20.7 0.1 collective-permute-start.5
  20.8 0.4 collective-permute-start.6
  21.3 0.0 collective-permute-done.7
  21.3 0.1 broadcast_select_fusion
  21.3 0.2 collective-permute-start.8
  21.5 1.1 %collective-permute-done.8.refs_11_ = bf16[3,2,4096]{2,1,0:T(2,128)(2,1)S(1)} collective-permute-done((bf16[3,2,4096]{2,1,0:T(2,128)(2,1)S(1)}, bf16[3,2,4096]{2,1,0:T(2,128)(2,1)S(1)}, u32[]{:S(2)}, u32[]{:S(2)}) %collective-permute-start.8) | collective-permute-done | bytes 49184 | tf_op jit(solution)/shard_map/ppermute | solution.py:474
  22.6 0.0 collective-permute-done.4.refs_5_
  22.6 0.0 collective-permute-done.5.refs_6_
  22.7 0.0 collective-permute-done.6.refs_7_
  22.7 4.8 %shard_map.102 = (bf16[512,128]{1,0:T(8,128)(2,1)}, bf16[16,4096]{1,0:T(8,128)(2,1)}, f32[8,128]{1,0:T(8,128)S(1)}, bf16[3,2,4096]{2,1,0:T(2,128)(2,1)}) custom-call(f32[32,512]{1,0:T(8,128)S(1)} %pad_maximum_fusion.refs_0_, f32[32,512]{1,0:T(8,128)S(1)} %collective-permute-done.refs_1_, f32[32,512]{1,0:T(8,128)S(1)} %collective-permute-done.1.refs_2_, ...), custom_call_target="tpu_custom_call" | custom-call | flops 16777216 | bytes 1048576 | tf_op jit(solution)/shard_map/pallas_call | solution.py:155
  27.6 0.6 copy-done.3
  28.2 9.8 %all-to-all-start = ((bf16[256,2,128]{2,1,0:T(2,128)(2,1)}), bf16[256,2,128]{2,1,0:T(2,128)(2,1)S(1)}, u32[]{:S(2)}, u32[]{:S(2)}) async-start(bf16[256,2,128]{2,1,0:T(2,128)(2,1)} %bitcast.2), calls=%async_computation | async-start | bytes 262144 | tf_op jit(solution)/shard_map/all_to_all | solution.py:519
  38.0 8.0 %shard_map.103 = (f32[128,2048]{1,0:T(8,128)}, bf16[128,2048]{1,0:T(8,128)(2,1)}, f32[128,2048]{1,0:T(8,128)}, f32[16,2048]{1,0:T(8,128)}) custom-call(f32[32,512]{1,0:T(8,128)} %copy-done, f32[32,512]{1,0:T(8,128)} %copy-done.3, f32[32,512]{1,0:T(8,128)} %copy-done.2, f32[32,512]{1,0:T(8,128)} %copy-done.1, f32[32,512]{1,0:T(8,128)} %copy-done.4, ...), custom_call_target="tpu_custom_call" | custom-call | flops 536870912 | bytes 1048576 | tf_op jit(solution)/shard_map/pallas_call | solution.py:380
  46.0 4.8 %all-to-all-done = bf16[256,2,128]{2,1,0:T(2,128)(2,1)S(1)} async-done(((bf16[256,2,128]{2,1,0:T(2,128)(2,1)}), bf16[256,2,128]{2,1,0:T(2,128)(2,1)S(1)}, u32[]{:S(2)}, u32[]{:S(2)}) %all-to-all-start) | async-done | bytes 131104 | tf_op jit(solution)/shard_map/all_to_all | solution.py:519
  50.8 1.2 %shard_map.104 = bf16[512,128]{1,0:T(8,128)(2,1)} custom-call(bf16[512,128]{1,0:T(8,128)(2,1)S(1)} %bitcast.8, f32[8,128]{1,0:T(8,128)S(1)} %get-tuple-element.43.decay_ref), custom_call_target="tpu_custom_call" | custom-call | flops 131072 | bytes 1048576 | tf_op jit(solution)/shard_map/pallas_call | solution.py:155
  52.0 9.0 %all-to-all-start.1 = ((bf16[256,2,128]{2,1,0:T(2,128)(2,1)}), bf16[256,2,128]{2,1,0:T(2,128)(2,1)S(1)}, u32[]{:S(2)}, u32[]{:S(2)}) async-start(bf16[256,2,128]{2,1,0:T(2,128)(2,1)} %bitcast.4), calls=%async_computation.1 | async-start | bytes 262144 | tf_op jit(solution)/shard_map/all_to_all | solution.py:519
  61.0 8.1 %shard_map.105 = (f32[128,2048]{1,0:T(8,128)}, bf16[128,2048]{1,0:T(8,128)(2,1)}, f32[128,2048]{1,0:T(8,128)}, f32[16,2048]{1,0:T(8,128)}) custom-call(f32[32,512]{1,0:T(8,128)} %copy-done, f32[32,512]{1,0:T(8,128)} %copy-done.3, f32[32,512]{1,0:T(8,128)} %copy-done.2, f32[32,512]{1,0:T(8,128)} %copy-done.1, f32[32,512]{1,0:T(8,128)} %copy-done.4, ...), custom_call_target="tpu_custom_call" | custom-call | flops 536870912 | bytes 1048576 | tf_op jit(solution)/shard_map/pallas_call | solution.py:380
  69.1 4.7 %all-to-all-done.1 = bf16[256,2,128]{2,1,0:T(2,128)(2,1)S(1)} async-done(((bf16[256,2,128]{2,1,0:T(2,128)(2,1)}), bf16[256,2,128]{2,1,0:T(2,128)(2,1)S(1)}, u32[]{:S(2)}, u32[]{:S(2)}) %all-to-all-start.1) | async-done | bytes 131104 | tf_op jit(solution)/shard_map/all_to_all | solution.py:519
  73.8 5.6 %shard_map.106 = bf16[128,4096]{1,0:T(8,128)(2,1)} custom-call(bf16[512,128]{1,0:T(8,128)(2,1)S(1)} %bitcast.7, bf16[16,4096]{1,0:T(8,128)(2,1)} %get-tuple-element.36.refs_9_.top_any, f32[1,4096]{1,0:T(1,128)} %bitcast.11, bf16[128,4096]{1,0:T(8,128)(2,1)} %shard_map.101.refs_8_.sig_any, f32[128,2048]{1,0:T(8,128)} %get-tuple-element.49.refs_0_, ...), custom_call_target="tpu_custom_call" | custom-call | flops 16777216 | bytes 1048576 | tf_op jit(solution)/shard_map/pallas_call | solution.py:155
  (17 shorter events, 0.0 us)
Async XLA Ops:
  0.8 21.9 %copy-start = (f32[32,512]{1,0:T(8,128)}, f32[32,512]{1,0:T(8,128)S(1)}, u32[]{:S(2)}) copy-start(f32[32,512]{1,0:T(8,128)S(1)} %pad_maximum_fusion.refs_0_) | copy-start | bytes 196612
  0.8 19.4 %collective-permute-start.2 = (f32[32,512]{1,0:T(8,128)S(1)}, f32[32,512]{1,0:T(8,128)S(1)}, u32[]{:S(2)}, u32[]{:S(2)}) collective-permute-start(f32[32,512]{1,0:T(8,128)S(1)} %pad_maximum_fusion.refs_0_), channel_id=1, source_target_pairs={{0,6},{1,7},{2,0},{3,1},{4,2},{5,3},{6,4},{7,5},{8,14},{9,15},{10,... | collective-permute-start | bytes 196616 | tf_op jit(solution)/shard_map/ppermute | solution.py:474
  7.7 12.5 %collective-permute-start.1 = (f32[32,512]{1,0:T(8,128)S(1)}, f32[32,512]{1,0:T(8,128)S(1)}, u32[]{:S(2)}, u32[]{:S(2)}) collective-permute-start(f32[32,512]{1,0:T(8,128)S(1)} %pad_maximum_fusion.refs_0_), channel_id=1, source_target_pairs={{0,132},{1,133},{2,134},{3,135},{4,128},{5,129},{6,130},{7,131},{8... | collective-permute-start | bytes 196616 | tf_op jit(solution)/shard_map/ppermute | solution.py:488
  10.1 10.1 %collective-permute-start = (f32[32,512]{1,0:T(8,128)S(1)}, f32[32,512]{1,0:T(8,128)S(1)}, u32[]{:S(2)}, u32[]{:S(2)}) collective-permute-start(f32[32,512]{1,0:T(8,128)S(1)} %pad_maximum_fusion.refs_0_), channel_id=1, source_target_pairs={{0,2},{1,3},{2,4},{3,5},{4,6},{5,7},{6,0},{7,1},{8,10},{9,11},{10,... | collective-permute-start | bytes 196616 | tf_op jit(solution)/shard_map/ppermute | solution.py:474
  12.3 9.0 %collective-permute-start.7 = (bf16[3,2,4096]{2,1,0:T(2,128)(2,1)}, bf16[3,2,4096]{2,1,0:T(2,128)(2,1)S(1)}, u32[]{:S(2)}, u32[]{:S(2)}) collective-permute-start(bf16[3,2,4096]{2,1,0:T(2,128)(2,1)} %shard_map.100), channel_id=1, source_target_pairs={{1,3},{3,5},{5,7},{7,9},{9,11},{11,13},{13,15},{15,17},{17,19},{19... | collective-permute-start | bytes 147464 | tf_op jit(solution)/shard_map/ppermute | solution.py:510
  16.6 4.9 %collective-permute-start.3 = (f32[32,512]{1,0:T(8,128)S(1)}, f32[32,512]{1,0:T(8,128)S(1)}, u32[]{:S(2)}, u32[]{:S(2)}) collective-permute-start(f32[32,512]{1,0:T(8,128)S(1)} %pad_maximum_fusion.refs_0_), channel_id=1, source_target_pairs={{0,1},{1,0},{2,3},{3,2},{4,5},{5,4},{6,7},{7,6},{8,9},{9,8},{10,11... | collective-permute-start | bytes 196616 | tf_op jit(solution)/shard_map/ppermute | solution.py:474
  16.7 4.5 %copy-start.8 = (bf16[3,2,4096]{2,1,0:T(2,128)(2,1)S(1)}, bf16[3,2,4096]{2,1,0:T(2,128)(2,1)}, u32[]{:S(2)}) copy-start(bf16[3,2,4096]{2,1,0:T(2,128)(2,1)} %shard_map.100) | copy-start | bytes 147460
  20.2 2.5 %copy-start.1 = (f32[32,512]{1,0:T(8,128)}, f32[32,512]{1,0:T(8,128)S(1)}, u32[]{:S(2)}) copy-start(f32[32,512]{1,0:T(8,128)S(1)} %collective-permute-done.2.refs_3_) | copy-start | bytes 196612
  20.2 2.5 %copy-start.2 = (f32[32,512]{1,0:T(8,128)}, f32[32,512]{1,0:T(8,128)S(1)}, u32[]{:S(2)}) copy-start(f32[32,512]{1,0:T(8,128)S(1)} %collective-permute-done.1.refs_2_) | copy-start | bytes 196612
  20.2 2.4 %collective-permute-start.4 = (f32[32,512]{1,0:T(8,128)S(1)}, f32[32,512]{1,0:T(8,128)S(1)}, u32[]{:S(2)}, u32[]{:S(2)}) collective-permute-start(f32[32,512]{1,0:T(8,128)S(1)} %collective-permute-done.refs_1_), channel_id=1, source_target_pairs={{0,1},{1,0},{2,3},{3,2},{4,5},{5,4},{6,7},{7,6},{8,9},{9,8},{10,11... | collective-permute-start | bytes 196616 | tf_op jit(solution)/shard_map/ppermute | solution.py:474
  20.7 1.9 %collective-permute-start.5 = (f32[32,512]{1,0:T(8,128)S(1)}, f32[32,512]{1,0:T(8,128)S(1)}, u32[]{:S(2)}, u32[]{:S(2)}) collective-permute-start(f32[32,512]{1,0:T(8,128)S(1)} %collective-permute-done.1.refs_2_), channel_id=1, source_target_pairs={{0,1},{1,0},{2,3},{3,2},{4,5},{5,4},{6,7},{7,6},{8,9},{9,8},{10,11... | collective-permute-start | bytes 196616 | tf_op jit(solution)/shard_map/ppermute | solution.py:474
  20.8 1.8 %collective-permute-start.6 = (f32[32,512]{1,0:T(8,128)S(1)}, f32[32,512]{1,0:T(8,128)S(1)}, u32[]{:S(2)}, u32[]{:S(2)}) collective-permute-start(f32[32,512]{1,0:T(8,128)S(1)} %collective-permute-done.2.refs_3_), channel_id=1, source_target_pairs={{0,1},{1,0},{2,3},{3,2},{4,5},{5,4},{6,7},{7,6},{8,9},{9,8},{10,11... | collective-permute-start | bytes 196616 | tf_op jit(solution)/shard_map/ppermute | solution.py:474
  21.3 1.3 %collective-permute-start.8 = (bf16[3,2,4096]{2,1,0:T(2,128)(2,1)S(1)}, bf16[3,2,4096]{2,1,0:T(2,128)(2,1)S(1)}, u32[]{:S(2)}, u32[]{:S(2)}) collective-permute-start(bf16[3,2,4096]{2,1,0:T(2,128)(2,1)S(1)} %broadcast_select_fusion), channel_id=1, source_target_pairs={{0,1},{1,0},{2,3},{3,2},{4,5},{5,4},{6,7},{7,6},{8,9},{9,8},{10,11... | collective-permute-start | bytes 147464 | tf_op jit(solution)/shard_map/ppermute | solution.py:474
  21.5 6.0 %copy-start.4 = (f32[32,512]{1,0:T(8,128)}, f32[32,512]{1,0:T(8,128)S(1)}, u32[]{:S(2)}) copy-start(f32[32,512]{1,0:T(8,128)S(1)} %collective-permute-done.3.refs_4_) | copy-start | bytes 196612
  22.6 4.9 %copy-start.5 = (f32[32,512]{1,0:T(8,128)}, f32[32,512]{1,0:T(8,128)S(1)}, u32[]{:S(2)}) copy-start(f32[32,512]{1,0:T(8,128)S(1)} %collective-permute-done.4.refs_5_) | copy-start | bytes 196612
  22.6 4.9 %copy-start.6 = (f32[32,512]{1,0:T(8,128)}, f32[32,512]{1,0:T(8,128)S(1)}, u32[]{:S(2)}) copy-start(f32[32,512]{1,0:T(8,128)S(1)} %collective-permute-done.5.refs_6_) | copy-start | bytes 196612
  22.7 4.8 %copy-start.7 = (f32[32,512]{1,0:T(8,128)}, f32[32,512]{1,0:T(8,128)S(1)}, u32[]{:S(2)}) copy-start(f32[32,512]{1,0:T(8,128)S(1)} %collective-permute-done.6.refs_7_) | copy-start | bytes 196612
  27.5 0.6 copy-start.3
  28.2 22.6 %all-to-all-start = ((bf16[256,2,128]{2,1,0:T(2,128)(2,1)}), bf16[256,2,128]{2,1,0:T(2,128)(2,1)S(1)}, u32[]{:S(2)}, u32[]{:S(2)}) async-start(bf16[256,2,128]{2,1,0:T(2,128)(2,1)} %bitcast.2), calls=%async_computation | async-start | bytes 262144 | tf_op jit(solution)/shard_map/all_to_all | solution.py:519
  52.0 21.8 %all-to-all-start.1 = ((bf16[256,2,128]{2,1,0:T(2,128)(2,1)}), bf16[256,2,128]{2,1,0:T(2,128)(2,1)S(1)}, u32[]{:S(2)}, u32[]{:S(2)}) async-start(bf16[256,2,128]{2,1,0:T(2,128)(2,1)} %bitcast.4), calls=%async_computation.1 | async-start | bytes 262144 | tf_op jit(solution)/shard_map/all_to_all | solution.py:519

commit v4 on v3

--- a/solution.py
+++ b/solution.py
@@ -193,9 +193,7 @@
 
 
 def fetch_params(mover, arrays, par0, par1):
-    return [
-        mover.start(array, (par0, par1)[n // NH].at[n % NH]) for n, array in enumerate(arrays)
-    ]
+    return [mover.start(array, par) for array, par in zip(arrays, (par0, par1))]
 
 
 def states(rates, first, second, sig_ref, at):
@@ -226,8 +224,8 @@
 
 
 def state_kernel(*refs):
-    pars, (sig_any, k_any, v_any, edge, filt_any, state_out, top_any, decay, edge_any) = refs[: 2 * NH], refs[2 * NH : 2 * NH + 9]
-    par0, par1, packed, k_top, v_top, filt, sig, top, state, sems = refs[2 * NH + 9 :]
+    pars, (sig_any, k_any, v_any, edge, filt_any, state_out, top_any, decay, edge_any, *par_anys) = refs[: 2 * NH], refs[2 * NH : 2 * NH + 11]
+    par0, par1, packed, k_top, v_top, filt, sig, top, state, sems = refs[2 * NH + 11 :]
     place = where_am_i()
     mover = Mover(sems)
     modes, group = par0.shape[1] // 2, par0.shape[2]
@@ -242,7 +240,7 @@
         (par0, par1)[n // NH][n % NH] = array[...]
     parts = [slice(at, at + group) for at in range(0, width, group)]
     signals = [mover.start(sig_any.at[:, at], packed.at[:, at]) for at in parts]
-    kept = mover.start(edge, edge_any)
+    kept = [mover.start(a, b) for a, b in ((edge, edge_any), (par0, par_anys[0]), (par1, par_anys[1]))]
     for copy in small:
         copy.wait()
     for n, at in enumerate(parts):
@@ -261,7 +259,8 @@
     decay[...] = own_decay(place, par0, par1, float(sig.shape[0]))
     state_out[...] = state[...].astype(BF16)
     sent.wait()
-    kept.wait()
+    for copy in kept:
+        copy.wait()
 
 
 def state_call(pars, sig, k_proj, v_proj, edges, filt):
@@ -272,14 +271,14 @@
     return run(
         state_kernel,
         *pars, sig, k_proj, v_proj, edges, filt,
-        out=[((count, LANE), BF16), ((16, width), BF16), ((8, LANE), F32), (edges.shape, BF16)],
+        out=[((count, LANE), BF16), ((16, width), BF16), ((8, LANE), F32), (edges.shape, BF16), par, par],
         scratch=[
             par, par, ((rows, width), BF16), ((16, width), BF16), ((16, width), BF16),
             ((2, 3, width), F32), ((rows, group), F32), ((16, width), BF16), ((count, LANE), F32),
         ],
         near=[*range(2 * NH), 2 * NH + 3],
         near_out=[0, 2],
-        copies=5 + width // group,
+        copies=7 + width // group,
         flops=rows * width * modes * 2,
     )
 
@@ -312,9 +311,9 @@
 
 
 def local_kernel(first, *refs):
-    sig_ref, top_ref, q_ref, edge_ref, filt_ref, fwd_ref, inv_ref, shift_ref = refs[2 * NH : 2 * NH + 8]
-    conv_ref, query_ref, term_ref, step_s = refs[2 * NH + 8 : 2 * NH + 12]
-    par0, par1, taps_ref, rate_s, decay_s, weight_s, sems = refs[2 * NH + 12 :]
+    sig_ref, top_ref, q_ref, edge_ref, filt_ref, fwd_ref, inv_ref, shift_ref = refs[2:10]
+    conv_ref, query_ref, term_ref, step_s = refs[10:14]
+    par0, par1, taps_ref, rate_s, decay_s, weight_s, sems = refs[14:]
     place = where_am_i()
     rows, group = sig_ref.shape
     modes = par0.shape[1] // 2
@@ -323,7 +322,7 @@
 
     @pl.when(pl.program_id(0) == 0)
     def _():
-        for copy in fetch_params(Mover(sems), refs[: 2 * NH], par0, par1):
+        for copy in fetch_params(Mover(sems), refs[:2], par0, par1):
             copy.wait()
 
     rate_s[...] = params_of(place, chip, parity, par0, par1, slice(0, modes))
@@ -366,8 +365,8 @@
 
 def local_call(half, pars, sig, top, q_proj, edges, filt, fwd, inv, shift):
     rows, width = q_proj.shape
-    modes, group = pars[0].shape[0] // 2, pars[0].shape[1]
-    par = pltpu.VMEM((NH, 2 * modes, group), F32)
+    modes, group = pars[0].shape[1] // 2, pars[0].shape[2]
+    par = pltpu.VMEM(pars[0].shape, F32)
     first = half * NH
 
     def lanes(n):
@@ -380,7 +379,7 @@
     return pl.pallas_call(
         functools.partial(local_kernel, first),
         grid=(NH,),
-        in_specs=[ANY] * (2 * NH) + [
+        in_specs=[ANY] * 2 + [
             pl.BlockSpec((rows, group), lanes), pl.BlockSpec((16, group), lanes), pl.BlockSpec((rows, group), lanes),
             pl.BlockSpec((3, 2, group), lambda n: (0, 0, n + first)), pl.BlockSpec((3, 3, group), lambda n: (0, 0, n + first)),
             whole(fwd), whole(inv), whole(shift),
@@ -393,7 +392,7 @@
             jax.ShapeDtypeStruct((modes, width // 2), F32),
         ],
         scratch_shapes=[par, par, pltpu.VMEM((rows, group), F32)]
-        + [pltpu.VMEM((modes, group), F32)] * 3 + [pltpu.SemaphoreType.DMA((2 * NH,))],
+        + [pltpu.VMEM((modes, group), F32)] * 3 + [pltpu.SemaphoreType.DMA((2,))],
         compiler_params=GRANT,
         cost_estimate=cost(rows * rows * group * 16 * NH),
     )(*pars, sig, top, q_proj, edges, filt, fwd, inv, shift)
@@ -513,7 +512,7 @@
     sig = signal_call(k_proj, v_proj, short_filter)
     mine = [own, one, far, three]
     pars = mine + [to_core(own)] + [to_core(after(value, sig)) for value in mine[1:]]
-    states, top, decay, edges = state_call(pars, sig, k_proj, v_proj, edges, short_filter)
+    states, top, decay, edges, *pars = state_call(pars, sig, k_proj, v_proj, edges, short_filter)
 
     def exchange(value):
         return lax.all_to_all(value, everyone, 0, 0, tiled=True)

time: 80 us -> 79.3 us (level)
  no operation moved by 1% of the time
where the time goes in v4:
time: 79.3 us; the launch traced here: 78.9 us
  starting transfers between devices  34.1 us (43%)
  Pallas kernels  32.8 us (41%)
  waiting for transfers between devices  10.9 us (14%)
  other arithmetic  0.83 us (1%)
    all_to_all x2, starting transfers between devices, exchange(): return lax.all_to_all(value, everyone, 0, 0, tiled=True)  18.7 us
    pallas_call x2, Pallas kernels, local_call(): pl.pallas_call(functools.partial(local_kernel, first), grid=(NH,), in_spe...  16 us
    pallas_call x4, Pallas kernels, run(): pl.pallas_call(kernel, in_specs=[VMEM if n in near else HBM for n in rang...  15.2 us
    ppermute x7, starting transfers between devices, moved(): return lax.ppermute(value, 'ch', [(i, target(i)) for i in range(2 * NH)])  10.4 us
    all_to_all x2, waiting for transfers between devices, exchange(): return lax.all_to_all(value, everyone, 0, 0, tiled=True)  9.72 us
    ppermute x1, starting transfers between devices, on_device(): lax.ppermute(edges, everyone, [(i, i + 2) for i in range(1, total - 2, 2)])  4.3 us
    pallas_call x1, Pallas kernels, edge_call(): pl.pallas_call(edge_kernel, in_specs=[ANY, ANY, ANY], out_specs=VMEM, out...  1.7 us
  transfers between devices with their start and end apart: 11, of which 3 were waited for; matrix products, arithmetic and copies ran while one was open for 0% of the time, Pallas kernels for 27%

profile of v4, /device:TPU:1, one launch (start us, length us, event | category | flops | bytes accessed | tf_op | source)
XLA Modules:
  0.0 78.9 jit_solution(16680909731159646115)
XLA Ops:
  0.0 0.8 pad_maximum_fusion.refs_0_
  0.8 6.8 %collective-permute-start.2 = (f32[32,512]{1,0:T(8,128)S(1)}, f32[32,512]{1,0:T(8,128)S(1)}, u32[]{:S(2)}, u32[]{:S(2)}) collective-permute-start(f32[32,512]{1,0:T(8,128)S(1)} %pad_maximum_fusion.refs_0_), channel_id=1, source_target_pairs={{0,6},{1,7},{2,0},{3,1},{4,2},{5,3},{6,4},{7,5},{8,14},{9,15},{10,... | collective-permute-start | bytes 196616 | tf_op jit(solution)/shard_map/ppermute | solution.py:473
  7.6 0.7 collective-permute-start.1
  8.3 1.7 %shard_map.100 = bf16[3,2,4096]{2,1,0:T(2,128)(2,1)} custom-call(bf16[128,4096]{1,0:T(8,128)(2,1)} %refs_4_.3, bf16[128,4096]{1,0:T(8,128)(2,1)} %refs_9_.3, bf16[128,4096]{1,0:T(8,128)(2,1)} %refs_10_.1), custom_call_target="tpu_custom_call" | custom-call | flops 1048576 | bytes 1048576 | tf_op jit(solution)/shard_map/pallas_call | solution.py:85
  10.1 2.2 %collective-permute-start = (f32[32,512]{1,0:T(8,128)S(1)}, f32[32,512]{1,0:T(8,128)S(1)}, u32[]{:S(2)}, u32[]{:S(2)}) collective-permute-start(f32[32,512]{1,0:T(8,128)S(1)} %pad_maximum_fusion.refs_0_), channel_id=1, source_target_pairs={{0,2},{1,3},{2,4},{3,5},{4,6},{5,7},{6,0},{7,1},{8,10},{9,11},{10,... | collective-permute-start | bytes 196616 | tf_op jit(solution)/shard_map/ppermute | solution.py:473
  12.2 4.3 %collective-permute-start.7 = (bf16[3,2,4096]{2,1,0:T(2,128)(2,1)}, bf16[3,2,4096]{2,1,0:T(2,128)(2,1)S(1)}, u32[]{:S(2)}, u32[]{:S(2)}) collective-permute-start(bf16[3,2,4096]{2,1,0:T(2,128)(2,1)} %shard_map.100), channel_id=1, source_target_pairs={{1,3},{3,5},{5,7},{7,9},{9,11},{11,13},{13,15},{15,17},{17,19},{19... | collective-permute-start | bytes 147464 | tf_op jit(solution)/shard_map/ppermute | solution.py:509
  16.5 0.1 collective-permute-start.3
  16.6 0.0 copy-start
  16.7 3.4 %shard_map.101.refs_8_.refs_2_.sig_any = bf16[128,4096]{1,0:T(8,128)(2,1)} custom-call(bf16[128,4096]{1,0:T(8,128)(2,1)} %refs_9_.3, bf16[128,4096]{1,0:T(8,128)(2,1)} %refs_10_.1, f32[3,3,4096]{2,1,0:T(4,128)} %refs_6_.3), custom_call_target="tpu_custom_call" | custom-call | flops 6291456 | bytes 1048576 | tf_op jit(solution)/shard_map/pallas_call | solution.py:155
  20.1 0.0 collective-permute-done.2.refs_3_
  20.1 0.0 collective-permute-done.1.refs_2_
  20.1 0.0 collective-permute-done.refs_1_
  20.1 0.5 collective-permute-start.4
  20.6 0.1 collective-permute-start.5
  20.7 0.4 collective-permute-start.6
  21.1 0.0 collective-permute-done.7
  21.2 0.1 broadcast_select_fusion
  21.2 0.2 collective-permute-start.8
  21.4 0.0 collective-permute-done.3.refs_4_
  21.4 1.1 %collective-permute-done.8.refs_11_ = bf16[3,2,4096]{2,1,0:T(2,128)(2,1)S(1)} collective-permute-done((bf16[3,2,4096]{2,1,0:T(2,128)(2,1)S(1)}, bf16[3,2,4096]{2,1,0:T(2,128)(2,1)S(1)}, u32[]{:S(2)}, u32[]{:S(2)}) %collective-permute-start.8) | collective-permute-done | bytes 49184 | tf_op jit(solution)/shard_map/ppermute | solution.py:473
  22.5 0.0 collective-permute-done.4.refs_5_
  22.5 0.0 collective-permute-done.5.refs_6_
  22.5 0.0 collective-permute-done.6.refs_7_
  22.5 5.0 %shard_map.102 = (bf16[512,128]{1,0:T(8,128)(2,1)}, bf16[16,4096]{1,0:T(8,128)(2,1)}, f32[8,128]{1,0:T(8,128)S(1)}, bf16[3,2,4096]{2,1,0:T(2,128)(2,1)}, f32[4,32,512]{2,1,0:T(8,128)}, /*index=5*/f32[4,32,512]{2,1,0:T(8,128)}) custom-call(f32[32,512]{1,0:T(8,128)S(1)} %pad_maximum_fusion.refs_0_, f32[32,512]{1,0:T(8,128)S(1)} %collective-permute-done.refs_1_, ...), custom_call_target="tpu_custom_call" | custom-call | flops 16777216 | bytes 1048576 | tf_op jit(solution)/shard_map/pallas_call | solution.py:155
  27.5 9.9 %all-to-all-start = ((bf16[256,2,128]{2,1,0:T(2,128)(2,1)}), bf16[256,2,128]{2,1,0:T(2,128)(2,1)S(1)}, u32[]{:S(2)}, u32[]{:S(2)}) async-start(bf16[256,2,128]{2,1,0:T(2,128)(2,1)} %bitcast.2), calls=%async_computation | async-start | bytes 262144 | tf_op jit(solution)/shard_map/all_to_all | solution.py:518
  37.4 7.9 %shard_map.103 = (f32[128,2048]{1,0:T(8,128)}, bf16[128,2048]{1,0:T(8,128)(2,1)}, f32[128,2048]{1,0:T(8,128)}, f32[16,2048]{1,0:T(8,128)}) custom-call(f32[4,32,512]{2,1,0:T(8,128)} %get-tuple-element.38.refs_0_, f32[4,32,512]{2,1,0:T(8,128)} %get-tuple-element.39.refs_1_, bf16[128,4096]{1,0:T(8,128)(2,1)} %shard_map.101.refs_8_.refs_2_.sig_any, ...), custom_call_target="tpu_custom_call" | custom-call | flops 536870912 | bytes 1048576 | tf_op jit(solution)/shard_map/pallas_call | solution.py:379
  45.4 4.9 %all-to-all-done = bf16[256,2,128]{2,1,0:T(2,128)(2,1)S(1)} async-done(((bf16[256,2,128]{2,1,0:T(2,128)(2,1)}), bf16[256,2,128]{2,1,0:T(2,128)(2,1)S(1)}, u32[]{:S(2)}, u32[]{:S(2)}) %all-to-all-start) | async-done | bytes 131104 | tf_op jit(solution)/shard_map/all_to_all | solution.py:518
  50.3 1.2 %shard_map.104 = bf16[512,128]{1,0:T(8,128)(2,1)} custom-call(bf16[512,128]{1,0:T(8,128)(2,1)S(1)} %bitcast.8, f32[8,128]{1,0:T(8,128)S(1)} %get-tuple-element.47.decay_ref), custom_call_target="tpu_custom_call" | custom-call | flops 131072 | bytes 1048576 | tf_op jit(solution)/shard_map/pallas_call | solution.py:155
  51.5 8.8 %all-to-all-start.1 = ((bf16[256,2,128]{2,1,0:T(2,128)(2,1)}), bf16[256,2,128]{2,1,0:T(2,128)(2,1)S(1)}, u32[]{:S(2)}, u32[]{:S(2)}) async-start(bf16[256,2,128]{2,1,0:T(2,128)(2,1)} %bitcast.4), calls=%async_computation.1 | async-start | bytes 262144 | tf_op jit(solution)/shard_map/all_to_all | solution.py:518
  60.3 8.0 %shard_map.105 = (f32[128,2048]{1,0:T(8,128)}, bf16[128,2048]{1,0:T(8,128)(2,1)}, f32[128,2048]{1,0:T(8,128)}, f32[16,2048]{1,0:T(8,128)}) custom-call(f32[4,32,512]{2,1,0:T(8,128)} %get-tuple-element.38.refs_0_, f32[4,32,512]{2,1,0:T(8,128)} %get-tuple-element.39.refs_1_, bf16[128,4096]{1,0:T(8,128)(2,1)} %shard_map.101.refs_8_.refs_2_.sig_any, ...), custom_call_target="tpu_custom_call" | custom-call | flops 536870912 | bytes 1048576 | tf_op jit(solution)/shard_map/pallas_call | solution.py:379
  68.4 4.8 %all-to-all-done.1 = bf16[256,2,128]{2,1,0:T(2,128)(2,1)S(1)} async-done(((bf16[256,2,128]{2,1,0:T(2,128)(2,1)}), bf16[256,2,128]{2,1,0:T(2,128)(2,1)S(1)}, u32[]{:S(2)}, u32[]{:S(2)}) %all-to-all-start.1) | async-done | bytes 131104 | tf_op jit(solution)/shard_map/all_to_all | solution.py:518
  73.2 5.6 %shard_map.106 = bf16[128,4096]{1,0:T(8,128)(2,1)} custom-call(bf16[512,128]{1,0:T(8,128)(2,1)S(1)} %bitcast.7, bf16[16,4096]{1,0:T(8,128)(2,1)} %get-tuple-element.40.refs_3_.top_any, f32[1,4096]{1,0:T(1,128)} %bitcast.11, bf16[128,4096]{1,0:T(8,128)(2,1)} %shard_map.101.refs_8_.refs_2_.sig_any, f32[128,2048]{1,0:T(8,128)} %get-tuple-element.53.refs_0_, ...), custom_call_target="tpu_custom_call" | custom-call | flops 16777216 | bytes 1048576 | tf_op jit(solution)/shard_map/pallas_call | solution.py:155
  (1 shorter events, 0.0 us)
Async XLA Ops:
  0.8 19.3 %collective-permute-start.2 = (f32[32,512]{1,0:T(8,128)S(1)}, f32[32,512]{1,0:T(8,128)S(1)}, u32[]{:S(2)}, u32[]{:S(2)}) collective-permute-start(f32[32,512]{1,0:T(8,128)S(1)} %pad_maximum_fusion.refs_0_), channel_id=1, source_target_pairs={{0,6},{1,7},{2,0},{3,1},{4,2},{5,3},{6,4},{7,5},{8,14},{9,15},{10,... | collective-permute-start | bytes 196616 | tf_op jit(solution)/shard_map/ppermute | solution.py:473
  7.6 12.4 %collective-permute-start.1 = (f32[32,512]{1,0:T(8,128)S(1)}, f32[32,512]{1,0:T(8,128)S(1)}, u32[]{:S(2)}, u32[]{:S(2)}) collective-permute-start(f32[32,512]{1,0:T(8,128)S(1)} %pad_maximum_fusion.refs_0_), channel_id=1, source_target_pairs={{0,132},{1,133},{2,134},{3,135},{4,128},{5,129},{6,130},{7,131},{8... | collective-permute-start | bytes 196616 | tf_op jit(solution)/shard_map/ppermute | solution.py:487
  10.1 10.0 %collective-permute-start = (f32[32,512]{1,0:T(8,128)S(1)}, f32[32,512]{1,0:T(8,128)S(1)}, u32[]{:S(2)}, u32[]{:S(2)}) collective-permute-start(f32[32,512]{1,0:T(8,128)S(1)} %pad_maximum_fusion.refs_0_), channel_id=1, source_target_pairs={{0,2},{1,3},{2,4},{3,5},{4,6},{5,7},{6,0},{7,1},{8,10},{9,11},{10,... | collective-permute-start | bytes 196616 | tf_op jit(solution)/shard_map/ppermute | solution.py:473
  12.2 8.9 %collective-permute-start.7 = (bf16[3,2,4096]{2,1,0:T(2,128)(2,1)}, bf16[3,2,4096]{2,1,0:T(2,128)(2,1)S(1)}, u32[]{:S(2)}, u32[]{:S(2)}) collective-permute-start(bf16[3,2,4096]{2,1,0:T(2,128)(2,1)} %shard_map.100), channel_id=1, source_target_pairs={{1,3},{3,5},{5,7},{7,9},{9,11},{11,13},{13,15},{15,17},{17,19},{19... | collective-permute-start | bytes 147464 | tf_op jit(solution)/shard_map/ppermute | solution.py:509
  16.5 4.9 %collective-permute-start.3 = (f32[32,512]{1,0:T(8,128)S(1)}, f32[32,512]{1,0:T(8,128)S(1)}, u32[]{:S(2)}, u32[]{:S(2)}) collective-permute-start(f32[32,512]{1,0:T(8,128)S(1)} %pad_maximum_fusion.refs_0_), channel_id=1, source_target_pairs={{0,1},{1,0},{2,3},{3,2},{4,5},{5,4},{6,7},{7,6},{8,9},{9,8},{10,11... | collective-permute-start | bytes 196616 | tf_op jit(solution)/shard_map/ppermute | solution.py:473
  16.6 4.5 %copy-start = (bf16[3,2,4096]{2,1,0:T(2,128)(2,1)S(1)}, bf16[3,2,4096]{2,1,0:T(2,128)(2,1)}, u32[]{:S(2)}) copy-start(bf16[3,2,4096]{2,1,0:T(2,128)(2,1)} %shard_map.100) | copy-start | bytes 147460
  20.1 2.4 %collective-permute-start.4 = (f32[32,512]{1,0:T(8,128)S(1)}, f32[32,512]{1,0:T(8,128)S(1)}, u32[]{:S(2)}, u32[]{:S(2)}) collective-permute-start(f32[32,512]{1,0:T(8,128)S(1)} %collective-permute-done.refs_1_), channel_id=1, source_target_pairs={{0,1},{1,0},{2,3},{3,2},{4,5},{5,4},{6,7},{7,6},{8,9},{9,8},{10,11... | collective-permute-start | bytes 196616 | tf_op jit(solution)/shard_map/ppermute | solution.py:473
  20.6 1.9 %collective-permute-start.5 = (f32[32,512]{1,0:T(8,128)S(1)}, f32[32,512]{1,0:T(8,128)S(1)}, u32[]{:S(2)}, u32[]{:S(2)}) collective-permute-start(f32[32,512]{1,0:T(8,128)S(1)} %collective-permute-done.1.refs_2_), channel_id=1, source_target_pairs={{0,1},{1,0},{2,3},{3,2},{4,5},{5,4},{6,7},{7,6},{8,9},{9,8},{10,11... | collective-permute-start | bytes 196616 | tf_op jit(solution)/shard_map/ppermute | solution.py:473
  20.7 1.8 %collective-permute-start.6 = (f32[32,512]{1,0:T(8,128)S(1)}, f32[32,512]{1,0:T(8,128)S(1)}, u32[]{:S(2)}, u32[]{:S(2)}) collective-permute-start(f32[32,512]{1,0:T(8,128)S(1)} %collective-permute-done.2.refs_3_), channel_id=1, source_target_pairs={{0,1},{1,0},{2,3},{3,2},{4,5},{5,4},{6,7},{7,6},{8,9},{9,8},{10,11... | collective-permute-start | bytes 196616 | tf_op jit(solution)/shard_map/ppermute | solution.py:473
  21.2 1.3 %collective-permute-start.8 = (bf16[3,2,4096]{2,1,0:T(2,128)(2,1)S(1)}, bf16[3,2,4096]{2,1,0:T(2,128)(2,1)S(1)}, u32[]{:S(2)}, u32[]{:S(2)}) collective-permute-start(bf16[3,2,4096]{2,1,0:T(2,128)(2,1)S(1)} %broadcast_select_fusion), channel_id=1, source_target_pairs={{0,1},{1,0},{2,3},{3,2},{4,5},{5,4},{6,7},{7,6},{8,9},{9,8},{10,11... | collective-permute-start | bytes 147464 | tf_op jit(solution)/shard_map/ppermute | solution.py:473
  27.5 22.7 %all-to-all-start = ((bf16[256,2,128]{2,1,0:T(2,128)(2,1)}), bf16[256,2,128]{2,1,0:T(2,128)(2,1)S(1)}, u32[]{:S(2)}, u32[]{:S(2)}) async-start(bf16[256,2,128]{2,1,0:T(2,128)(2,1)} %bitcast.2), calls=%async_computation | async-start | bytes 262144 | tf_op jit(solution)/shard_map/all_to_all | solution.py:518
  51.5 21.7 %all-to-all-start.1 = ((bf16[256,2,128]{2,1,0:T(2,128)(2,1)}), bf16[256,2,128]{2,1,0:T(2,128)(2,1)S(1)}, u32[]{:S(2)}, u32[]{:S(2)}) async-start(bf16[256,2,128]{2,1,0:T(2,128)(2,1)} %bitcast.4), calls=%async_computation.1 | async-start | bytes 262144 | tf_op jit(solution)/shard_map/all_to_all | solution.py:518
